TPU v7x, 512 devices: a whole 4x4x16 slice. The times are simulated.
512 devices in a mesh: gz: 16 (over z), row: 32 (over y, x, core).
Axes of the slice: x: 4, y: 4, z: 16, core: 2. Of those that a mesh axis runs over, the one named last changes fastest.
Arguments:
- rhs_local: float32 [8, 8, 8, 131072], P(None, None, None, ('gz', 'row')), may hold values from -10 to 10
- stretch: float32 [3, 131072], P(None, ('gz', 'row')), may hold values from 0.25 to 4
Outputs:
- precond: float32 [8, 8, 8, 131072], P(None, None, None, ('gz', 'row'))
All inputs are finite; a program needn't handle non-finite values.
Results may differ from a plain program's by a relative error of at most 0.0003.
Values sent between devices are 32-bit elements; how exact they have to be, the bound alone decides.
A program may use at most 128 MiB of HBM per device.

v0:
```python
import math

import jax
import jax.numpy as jnp
from jax import lax
from jax.sharding import PartitionSpec as P

ORDER = 7
MID = 3
ITERS = 5
EZ = 4
EA = 4
ER = 16


LOW_BOUND = 0.4
HIGH_BOUND = 4.0
HIGHEST = lax.Precision.HIGHEST


def with_halo(cells, sides, width):
    for axis, dim in sides:
        count = lax.axis_size(axis)
        head = lax.slice_in_dim(cells, 0, width, axis=dim)
        tail = lax.slice_in_dim(cells, cells.shape[dim] - width, cells.shape[dim], axis=dim)
        cells = jnp.concatenate(
            [
                lax.ppermute(tail, axis, [(i, (i + 1) % count) for i in range(count)]),
                cells,
                lax.ppermute(head, axis, [((i + 1) % count, i) for i in range(count)]),
            ],
            axis=dim,
        )
    return cells


def node_points(order):
    steps = jnp.arange(order + 1).astype(jnp.float32)
    return -jnp.cos(steps * (math.pi / order))


def level_tables(order):
    points = node_points(order)
    count = order + 1
    identity = jnp.eye(count, dtype=jnp.float32)
    distance = points[:, None] - points[None, :] + identity
    barycentric = 1.0 / jnp.prod(distance, axis=1)
    offdiag = barycentric[None, :] / barycentric[:, None] / distance * (1.0 - identity)
    derivative = offdiag - jnp.diag(jnp.sum(offdiag, axis=1))
    place = jnp.arange(count).astype(jnp.float32)
    running = jnp.ones((count,), jnp.float32)
    for freq in range(1, order // 2 + 1):
        factor = 2.0
        running = running - factor / (4.0 * freq * freq - 1.0) * jnp.cos(
            2.0 * freq * place * math.pi / order
        )
    endpoint = jnp.where((place == 0) | (place == order), 1.0, 2.0).astype(jnp.float32)
    weights = endpoint / order * running
    stiffness = jnp.dot(derivative.T * weights[None, :], derivative, precision=HIGHEST)
    return (weights, stiffness)


def interpolation(fine_order, coarse_order):
    fine_points = node_points(fine_order)
    coarse_points = node_points(coarse_order)
    columns = []
    for column in range(coarse_order + 1):
        value = jnp.ones((fine_order + 1,), jnp.float32)
        for other in range(coarse_order + 1):
            if other != column:
                value = (
                    value
                    * (fine_points - coarse_points[other])
                    / (coarse_points[column] - coarse_points[other])
                )
        columns.append(value)
    return jnp.stack(columns, axis=1)


def weight_shape(values, position, ndim):
    shape = [1] * ndim
    shape[position] = values.shape[0]
    return values.reshape(shape)


def element_apply(field, coeff, weights, stiffness):
    ndim = field.ndim
    along_z = weight_shape(weights, 0, ndim)
    along_a = weight_shape(weights, 1, ndim)
    along_r = weight_shape(weights, 2, ndim)
    part_z = jnp.einsum("ij,jbc...->ibc...", stiffness, field, precision=HIGHEST)
    part_a = jnp.einsum("ij,ajc...->aic...", stiffness, field, precision=HIGHEST)
    part_r = jnp.einsum("ij,abj...->abi...", stiffness, field, precision=HIGHEST)
    return (
        coeff[0] * along_a * along_r * part_z
        + coeff[1] * along_z * along_r * part_a
        + coeff[2] * along_z * along_a * part_r
    )


def element_diagonal(coeff, weights, stiffness, ndim):
    diag_k = jnp.diagonal(stiffness)
    term_z = (
        weight_shape(diag_k, 0, ndim)
        * weight_shape(weights, 1, ndim)
        * weight_shape(weights, 2, ndim)
    )
    term_a = (
        weight_shape(weights, 0, ndim)
        * weight_shape(diag_k, 1, ndim)
        * weight_shape(weights, 2, ndim)
    )
    term_r = (
        weight_shape(weights, 0, ndim)
        * weight_shape(weights, 1, ndim)
        * weight_shape(diag_k, 2, ndim)
    )
    return coeff[0] * term_z + coeff[1] * term_a + coeff[2] * term_r


def face_add(field, node_dim, stride, count, direction_kind):
    size = field.shape[0]
    moved = jnp.moveaxis(field, node_dim, 0)
    low_face = moved[0]
    high_face = moved[size - 1]
    elems = low_face.shape[-1]
    position = jnp.arange(elems) // stride % count
    zero_block = jnp.zeros(low_face.shape[:-1] + (stride,), jnp.float32)
    below_local = jnp.concatenate([zero_block, high_face[..., : elems - stride]], axis=-1)
    above_local = jnp.concatenate([low_face[..., stride:], zero_block], axis=-1)
    if direction_kind == "radial":
        from_below = jnp.where(position > 0, below_local, 0.0)
        from_above = jnp.where(position < count - 1, above_local, 0.0)
    else:
        outer = elems // (stride * count)
        split_shape = low_face.shape[:-1] + (outer, count, stride)
        low_edge = low_face.reshape(split_shape)[..., 0, :]
        high_edge = high_face.reshape(split_shape)[..., count - 1, :]
        stacked = jnp.stack([low_edge, high_edge], axis=0)
        if direction_kind == "azimuth":
            padded = with_halo(stacked, (("row", 0),), 1)
        else:
            padded = with_halo(stacked, (("gz", 0),), 1)
        remote_below = jnp.broadcast_to(padded[0][..., None, :], split_shape).reshape(
            low_face.shape
        )
        remote_above = jnp.broadcast_to(padded[3][..., None, :], split_shape).reshape(
            low_face.shape
        )
        from_below = jnp.where(position == 0, remote_below, below_local)
        from_above = jnp.where(position == count - 1, remote_above, above_local)
    moved = moved.at[0].set(low_face + from_below)
    moved = moved.at[size - 1].set(high_face + from_above)
    return jnp.moveaxis(moved, 0, node_dim)


def assemble(field):
    field = face_add(field, 2, 1, ER, "radial")
    field = face_add(field, 1, ER, EA, "azimuth")
    return face_add(field, 0, EA * ER, EZ, "axial")


def level_data(order):
    weights, stiffness = level_tables(order)
    count = order + 1
    node_index = jnp.arange(count)
    radial = jnp.arange(EZ * EA * ER) % ER
    at_wall = (node_index[:, None] == 0) & (radial[None, :] == 0) | (
        node_index[:, None] == count - 1
    ) & (radial[None, :] == ER - 1)
    wall_mask = jnp.where(at_wall, 0.0, 1.0).astype(jnp.float32)[None, None]
    edge = jnp.where((node_index == 0) | (node_index == count - 1), 0.5, 1.0).astype(jnp.float32)
    share = (edge[:, None, None] * edge[None, :, None] * edge[None, None, :])[..., None]
    return (weights, stiffness, wall_mask, share)


def chebyshev(operate, inverse_diag, rhs):
    theta = 0.5 * (HIGH_BOUND + LOW_BOUND)
    delta = 0.5 * (HIGH_BOUND - LOW_BOUND)
    rho_now = delta / theta
    step = inverse_diag * rhs / theta
    solution = step
    residual = rhs - operate(step)
    rho_next = 1.0 / (2.0 * theta / delta - rho_now)
    step = rho_next * rho_now * step + 2.0 * rho_next / delta * inverse_diag * residual
    return (solution + step, step, residual)


def restrict(field, table):
    return jnp.einsum("ia,jb,kc,ijke->abce", table, table, table, field, precision=HIGHEST)


def prolong(field, table):
    return jnp.einsum("ia,jb,kc,abce->ijke", table, table, table, field, precision=HIGHEST)


def coarse_spread(low_b, low_op, weight):

    def squared_norm(values):
        return lax.psum(jnp.sum(weight * values * values), ("gz", "row"))

    low_sol = jnp.zeros_like(low_b)
    low_res = low_b
    direction = low_b
    norm_now = squared_norm(low_res)
    for iteration in range(ITERS):
        image = low_op(direction)
        alpha = norm_now / lax.psum(jnp.sum(weight * direction * image), ("gz", "row"))
        low_sol = low_sol + alpha * direction
        low_res = low_res - alpha * image
        norm_next = squared_norm(low_res)
        direction = low_res + norm_next / norm_now * direction
        norm_now = norm_next
    return low_sol


def per_device(rhs_local, stretch):
    fine_tab = level_data(ORDER)
    mid_tab = level_data(MID)
    low_tab = level_data(1)

    def make_operator(tables):

        def operate(field):
            return tables[2] * assemble(element_apply(field, stretch, tables[0], tables[1]))

        return operate

    fine_op = make_operator(fine_tab)
    mid_op = make_operator(mid_tab)
    low_op = make_operator(low_tab)
    fine_inv = fine_tab[2] / assemble(element_diagonal(stretch, fine_tab[0], fine_tab[1], 4))
    mid_inv = mid_tab[2] / assemble(element_diagonal(stretch, mid_tab[0], mid_tab[1], 4))
    to_mid = interpolation(ORDER, MID)
    to_low = interpolation(MID, 1)
    fine_b = fine_tab[2] * assemble(rhs_local)
    fine_sol, fine_step, fine_res = chebyshev(fine_op, fine_inv, fine_b)
    fine_res = fine_res - fine_op(fine_step)
    mid_b = mid_tab[2] * assemble(restrict(fine_tab[3] * fine_res, to_mid))
    mid_sol, mid_step, mid_res = chebyshev(mid_op, mid_inv, mid_b)
    mid_res = mid_res - mid_op(mid_step)
    low_b = low_tab[2] * assemble(restrict(mid_tab[3] * mid_res, to_low))
    low_sol = coarse_spread(low_b, low_op, low_tab[2] * low_tab[3])
    lifted = prolong(low_sol, to_low)
    mid_sol = mid_sol + lifted
    mid_res = mid_res - mid_op(lifted)
    mid_sol = mid_sol + chebyshev(mid_op, mid_inv, mid_res)[0]
    raised = prolong(mid_sol, to_mid)
    fine_sol = fine_sol + raised
    fine_res = fine_res - fine_op(raised)
    return fine_sol + chebyshev(fine_op, fine_inv, fine_res)[0]


def solution(mesh):
    placed = (P(None, None, None, ("gz", "row")), P(None, ("gz", "row")))
    return jax.shard_map(
        per_device,
        mesh=mesh,
        in_specs=placed,
        out_specs=P(None, None, None, ("gz", "row")),
        check_vma=False,
    )
```

profile of v0, /device:TPU:1, one launch (start us, length us, event | category | flops | bytes accessed | tf_op | source)
XLA Modules:
  0.0 1453.8 jit_solution(4152309490251370697)
XLA Ops:
  6.0 4.5 collective-permute-start
  11.6 6.2 collective-permute-start.1
  23.2 6.9 collective-permute-start.5
  47.0 5.8 collective-permute-start.3
  55.1 5.0 collective-permute-start.7
  80.0 7.5 collective-permute-start.9
  98.8 4.7 collective-permute-start.11
  124.5 9.2 collective-permute-start.17
  146.8 5.2 collective-permute-start.19
  165.9 7.2 collective-permute-start.21
  173.3 7.0 collective-permute-start.13
  187.1 4.6 collective-permute-start.23
  193.9 4.6 collective-permute-start.15
  202.0 5.6 collective-permute-start.24
  207.9 5.2 collective-permute-start.25
  216.8 5.1 collective-permute-start.27
  230.1 7.8 collective-permute-start.29
  241.2 4.6 collective-permute-start.31
  248.7 8.8 collective-permute-start.33
  259.8 4.3 collective-permute-done.32
  264.5 4.8 collective-permute-start.35
  271.5 3.4 collective-permute-done.34
  279.5 8.9 collective-permute-start.37
  291.6 3.4 collective-permute-start.38
  297.9 107.6 %all-reduce.108 = (f32[]{:T(128)}, f32[]{:T(128)}) all-reduce(f32[]{:T(128)} %get-tuple-element.1302, f32[]{:T(128)} %get-tuple-element.1301), channel_id=1, replica_groups=mesh['gz'=16,'row'=32] {'gz','row'}, use_global_device_ids=true, to_apply=%region_5.6 | all-reduce | flops 2 | bytes 16 | tf_op jit(solution)/shard_map/psum | solution.py:200
  407.5 100.3 %psum.72 = f32[]{:T(128)} all-reduce(f32[]{:T(128)} %get-tuple-element.1311), channel_id=1, replica_groups=mesh['gz'=16,'row'=32] {'gz','row'}, use_global_device_ids=true, to_apply=%region_11.12 | all-reduce | flops 1 | bytes 8 | tf_op jit(solution)/shard_map/psum | solution.py:200
  514.8 3.1 collective-permute-done.41
  527.6 104.7 %psum.73 = f32[]{:T(128)} all-reduce(f32[]{:T(128)} %multiply_reduce_fusion.3), channel_id=1, replica_groups=mesh['gz'=16,'row'=32] {'gz','row'}, use_global_device_ids=true, to_apply=%region_13.14 | all-reduce | flops 1 | bytes 8 | tf_op jit(solution)/shard_map/psum | solution.py:208
  634.2 99.4 %psum.74 = f32[]{:T(128)} all-reduce(f32[]{:T(128)} %get-tuple-element.1309), channel_id=1, replica_groups=mesh['gz'=16,'row'=32] {'gz','row'}, use_global_device_ids=true, to_apply=%region_15.16 | all-reduce | flops 1 | bytes 8 | tf_op jit(solution)/shard_map/psum | solution.py:200
  736.9 2.9 collective-permute-start.44
  755.0 104.2 %psum.75 = f32[]{:T(128)} all-reduce(f32[]{:T(128)} %multiply_reduce_fusion.2), channel_id=1, replica_groups=mesh['gz'=16,'row'=32] {'gz','row'}, use_global_device_ids=true, to_apply=%region_17.18 | all-reduce | flops 1 | bytes 8 | tf_op jit(solution)/shard_map/psum | solution.py:208
  861.0 99.4 %psum.76 = f32[]{:T(128)} all-reduce(f32[]{:T(128)} %get-tuple-element.1307), channel_id=1, replica_groups=mesh['gz'=16,'row'=32] {'gz','row'}, use_global_device_ids=true, to_apply=%region_19.20 | all-reduce | flops 1 | bytes 8 | tf_op jit(solution)/shard_map/psum | solution.py:200
  963.7 2.9 collective-permute-start.48
  969.0 3.1 collective-permute-done.49
  978.0 2.9 collective-permute-done.50
  981.8 104.2 %psum.77 = f32[]{:T(128)} all-reduce(f32[]{:T(128)} %get-tuple-element.1305), channel_id=1, replica_groups=mesh['gz'=16,'row'=32] {'gz','row'}, use_global_device_ids=true, to_apply=%region_21.22 | all-reduce | flops 1 | bytes 8 | tf_op jit(solution)/shard_map/psum | solution.py:208
  1088.0 99.4 %psum.78 = f32[]{:T(128)} all-reduce(f32[]{:T(128)} %fusion.101), channel_id=1, replica_groups=mesh['gz'=16,'row'=32] {'gz','row'}, use_global_device_ids=true, to_apply=%region_23.24 | all-reduce | flops 1 | bytes 8 | tf_op jit(solution)/shard_map/psum | solution.py:200
  1194.9 3.1 collective-permute-done.53
  1207.6 104.2 %psum.79 = f32[]{:T(128)} all-reduce(f32[]{:T(128)} %multiply_reduce_fusion), channel_id=1, replica_groups=mesh['gz'=16,'row'=32] {'gz','row'}, use_global_device_ids=true, to_apply=%region_25.26 | all-reduce | flops 1 | bytes 8 | tf_op jit(solution)/shard_map/psum | solution.py:208
  1317.4 3.1 collective-permute-start.57
  1323.2 3.7 collective-permute-start.58
  1333.1 3.3 collective-permute-start.60
  1336.8 6.5 collective-permute-start.61
  1346.6 4.6 collective-permute-start.63
  1366.6 8.8 collective-permute-start.65
  1391.0 5.3 collective-permute-start.67
  1415.5 7.8 collective-permute-start.69
  1438.2 4.3 collective-permute-start.71
  (1037 shorter events, 291.4 us)
Async XLA Ops:
  6.0 34.9 %collective-permute-start = (f32[1,8,8,4,16]{4,3,2,1,0:T(4,128)}, f32[1,8,8,4,16]{4,3,2,1,0:T(4,128)S(1)}, u32[]{:S(2)}, u32[]{:S(2)}) collective-permute-start(f32[1,8,8,4,16]{4,3,2,1,0:T(4,128)} %bitcast.9), channel_id=1, source_target_pairs={{0,1},{1,2},{2,3},{3,4},{4,5},{5,6},{6,7},{7,8},{8,9},{9,10},{10,1... | collective-permute-start | bytes 49160 | tf_op jit(solution)/shard_map/ppermute | solution.py:28
  11.6 28.7 %collective-permute-start.1 = (f32[1,8,8,4,16]{4,3,2,1,0:T(4,128)}, f32[1,8,8,4,16]{4,3,2,1,0:T(4,128)S(1)}, u32[]{:S(2)}, u32[]{:S(2)}) collective-permute-start(f32[1,8,8,4,16]{4,3,2,1,0:T(4,128)} %bitcast.13), channel_id=1, source_target_pairs={{1,0},{2,1},{3,2},{4,3},{5,4},{6,5},{7,6},{8,7},{9,8},{10,9},{11,1... | collective-permute-start | bytes 49160 | tf_op jit(solution)/shard_map/ppermute | solution.py:30
  20.2 21.3 %collective-permute-start.4 = (f32[1,8,8,4,16]{4,3,2,1,0:T(4,128)}, f32[1,8,8,4,16]{4,3,2,1,0:T(4,128)}, u32[]{:S(2)}, u32[]{:S(2)}) collective-permute-start(f32[1,8,8,4,16]{4,3,2,1,0:T(4,128)} %bitcast.30), channel_id=1, source_target_pairs={{0,1},{1,2},{2,3},{3,4},{4,5},{5,6},{6,7},{7,8},{8,9},{9,10},{10,1... | collective-permute-start | bytes 49160 | tf_op jit(solution)/shard_map/ppermute | solution.py:28
  23.2 19.7 %collective-permute-start.5 = (f32[1,8,8,4,16]{4,3,2,1,0:T(4,128)}, f32[1,8,8,4,16]{4,3,2,1,0:T(4,128)S(1)}, u32[]{:S(2)}, u32[]{:S(2)}) collective-permute-start(f32[1,8,8,4,16]{4,3,2,1,0:T(4,128)} %bitcast.34), channel_id=1, source_target_pairs={{1,0},{2,1},{3,2},{4,3},{5,4},{6,5},{7,6},{8,7},{9,8},{10,9},{11,1... | collective-permute-start | bytes 49160 | tf_op jit(solution)/shard_map/ppermute | solution.py:30
  44.9 19.2 %collective-permute-start.2 = (f32[1,8,8,1,64]{4,1,2,3,0:T(8,128)S(1)}, f32[1,8,8,1,64]{4,1,2,3,0:T(8,128)S(1)}, u32[]{:S(2)}, u32[]{:S(2)}) collective-permute-start(f32[1,8,8,1,64]{4,1,2,3,0:T(8,128)S(1)} %bitcast.1489), channel_id=1, source_target_pairs={{0,32},{32,64},{64,96},{96,128},{128,160},{160,192},{192,224},{224... | collective-permute-start | bytes 49160 | tf_op jit(solution)/shard_map/ppermute | solution.py:28
  47.0 17.3 %collective-permute-start.3 = (f32[1,8,8,1,64]{4,1,2,3,0:T(8,128)S(1)}, f32[1,8,8,1,64]{4,1,2,3,0:T(8,128)S(1)}, u32[]{:S(2)}, u32[]{:S(2)}) collective-permute-start(f32[1,8,8,1,64]{4,1,2,3,0:T(8,128)S(1)} %bitcast.1488), channel_id=1, source_target_pairs={{32,0},{64,32},{96,64},{128,96},{160,128},{192,160},{224,192},{256... | collective-permute-start | bytes 49160 | tf_op jit(solution)/shard_map/ppermute | solution.py:30
  53.0 11.4 collective-permute-start.6
  55.1 9.5 collective-permute-start.7
  70.7 16.8 %collective-permute-start.8 = (f32[1,8,8,4,16]{4,3,2,1,0:T(4,128)}, f32[1,8,8,4,16]{4,3,2,1,0:T(4,128)S(1)}, u32[]{:S(2)}, u32[]{:S(2)}) collective-permute-start(f32[1,8,8,4,16]{4,3,2,1,0:T(4,128)} %bitcast.58), channel_id=1, source_target_pairs={{0,1},{1,2},{2,3},{3,4},{4,5},{5,6},{6,7},{7,8},{8,9},{9,10},{10,1... | collective-permute-start | bytes 49160 | tf_op jit(solution)/shard_map/ppermute | solution.py:28
  80.0 8.8 collective-permute-start.9
  90.6 13.0 collective-permute-start.10
  98.8 5.9 collective-permute-start.11
  113.9 19.8 %collective-permute-start.16 = (f32[1,8,8,4,16]{4,3,2,1,0:T(4,128)}, f32[1,8,8,4,16]{4,3,2,1,0:T(4,128)}, u32[]{:S(2)}, u32[]{:S(2)}) collective-permute-start(f32[1,8,8,4,16]{4,3,2,1,0:T(4,128)} %bitcast.104), channel_id=1, source_target_pairs={{0,1},{1,2},{2,3},{3,4},{4,5},{5,6},{6,7},{7,8},{8,9},{9,10},{10,1... | collective-permute-start | bytes 49160 | tf_op jit(solution)/shard_map/ppermute | solution.py:28
  124.5 13.5 collective-permute-start.17
  142.7 9.3 collective-permute-start.18
  146.8 8.5 collective-permute-start.19
  163.5 18.9 %collective-permute-start.12 = (f32[1,4,4,4,16]{4,3,2,1,0:T(4,128)S(1)}, f32[1,4,4,4,16]{4,3,2,1,0:T(4,128)S(1)}, u32[]{:S(2)}, u32[]{:S(2)}) collective-permute-start(f32[1,4,4,4,16]{4,3,2,1,0:T(4,128)S(1)} %bitcast.1490), channel_id=1, source_target_pairs={{0,1},{1,2},{2,3},{3,4},{4,5},{5,6},{6,7},{7,8},{8,9},{9,10},{10,1... | collective-permute-start | bytes 12296 | tf_op jit(solution)/shard_map/ppermute | solution.py:28
  165.9 17.4 %collective-permute-start.21 = (f32[1,4,4,4,16]{4,3,2,1,0:T(4,128)S(1)}, f32[1,4,4,4,16]{4,3,2,1,0:T(4,128)S(1)}, u32[]{:S(2)}, u32[]{:S(2)}) collective-permute-start(f32[1,4,4,4,16]{4,3,2,1,0:T(4,128)S(1)} %bitcast.1495), channel_id=1, source_target_pairs={{1,0},{2,1},{3,2},{4,3},{5,4},{6,5},{7,6},{8,7},{9,8},{10,9},{11,1... | collective-permute-start | bytes 12296 | tf_op jit(solution)/shard_map/ppermute | solution.py:30
  173.3 10.2 collective-permute-start.13
  184.7 13.7 collective-permute-start.22
  187.1 11.6 collective-permute-start.23
  191.8 6.9 collective-permute-start.14
  202.0 11.9 collective-permute-start.24
  207.9 6.3 collective-permute-start.25
  214.7 10.3 collective-permute-start.26
  216.8 8.3 collective-permute-start.27
  226.7 11.2 collective-permute-start.28
  230.1 8.6 collective-permute-start.29
  239.1 6.7 collective-permute-start.30
  248.7 11.0 collective-permute-start.33
  257.6 6.5 collective-permute-start.32
  264.5 6.9 collective-permute-start.35
  269.4 5.5 collective-permute-start.34
  277.3 11.2 collective-permute-start.36
  279.5 9.7 collective-permute-start.37
  521.3 5.5 collective-permute-start.42
  1323.2 6.7 collective-permute-start.58
  1333.1 10.1 collective-permute-start.60
  1336.8 7.3 collective-permute-start.61
  1344.4 6.7 collective-permute-start.62
  1361.7 14.4 collective-permute-start.64
  1366.6 12.8 collective-permute-start.65
  1388.9 7.5 collective-permute-start.66
  1391.0 6.1 collective-permute-start.67
  1410.5 12.8 collective-permute-start.68
  1415.5 12.4 collective-permute-start.69
  1434.1 8.5 collective-permute-start.70
  1438.2 8.4 collective-permute-start.71
  (84 other events, 716.9 us)
where the time goes:
time: 1470 us; the launch traced here: 1450 us
  blocking collectives  923 us (63%)
  starting transfers between devices  271 us (18%)
  local copies, waits for them, and re-layouts  125 us (9%)
  waiting for transfers between devices  40.9 us (3%)
  other arithmetic  38.8 us (3%)
  between operations  33.2 us (2%)
  matrix products  21.9 us (1%)
    psum x5, blocking collectives, squared_norm(): return lax.psum(jnp.sum(weight * values * values), ('gz', 'row'))  506 us
    psum x4, blocking collectives, coarse_spread(): lax.psum(jnp.sum(weight * direction * image), ('gz', 'row'))  417 us
    ppermute x36, starting transfers between devices, with_halo(): lax.ppermute(head, axis, [((i + 1) % count, i) for i in range(count)])  183 us
    ppermute x36, starting transfers between devices, with_halo(): lax.ppermute(tail, axis, [(i, (i + 1) % count) for i in range(count)])  87.4 us
  transfers between devices with their start and end apart: 72, of which 21 were waited for; matrix products, arithmetic and copies ran while one was open for 5% of the time, Pallas kernels for 0%

commit v1 on v0

v1 whole, which is shorter than its diff:
```python
import functools

import numpy as np

import jax
import jax.numpy as jnp
from jax import lax
from jax.experimental import pallas as pl
from jax.experimental.pallas import tpu as pltpu
from jax.sharding import PartitionSpec as P

ORDER = 7
MID = 3
ITERS = 5
EZ = 4
EA = 4
ER = 16
LANES = 128

LOW_BOUND = 0.4
HIGH_BOUND = 4.0
THETA = 0.5 * (HIGH_BOUND + LOW_BOUND)
DELTA = 0.5 * (HIGH_BOUND - LOW_BOUND)
RHO = DELTA / THETA
RHO2 = 1.0 / (2.0 * THETA / DELTA - RHO)

DIRS = ((0, 1), (0, -1), (1, 0), (-1, 0), (1, 1), (1, -1), (-1, 1), (-1, -1))
ROUNDS = ((8, 8, 4), (8,), (8,), (4,), (4,), (4,), (2,), (2,), (2,), (2,), (2,), (4,), (4,), (8,), (8,))


def points_of(order):
    return -np.cos(np.pi * np.arange(order + 1) / order)


def tables_of(order):
    x = points_of(order)
    n = order + 1
    place = np.arange(n)
    running = np.ones(n)
    for j in range(1, order // 2 + 1):
        b = 1.0 if 2 * j == order else 2.0
        running = running - b * np.cos(2 * np.pi * j * place / order) / (4 * j * j - 1)
    weights = np.where((place == 0) | (place == order), 1.0, 2.0) / order * running
    gap = x[:, None] - x[None, :] + np.eye(n)
    bary = 1.0 / np.prod(gap, axis=1)
    deriv = bary[None, :] / bary[:, None] / gap * (1.0 - np.eye(n))
    deriv = deriv - np.diag(deriv.sum(axis=1))
    stiff = deriv.T @ (weights[:, None] * deriv)
    return weights, stiff / weights[:, None]


def interpolation(fine_order, coarse_order):
    x = points_of(fine_order)
    y = points_of(coarse_order)
    table = np.ones((fine_order + 1, coarse_order + 1))
    for j in range(coarse_order + 1):
        for k in range(coarse_order + 1):
            if k != j:
                table[:, j] *= (x - y[k]) / (y[j] - y[k])
    return table


def shared(table):
    out = table.copy()
    out[0] *= 0.5
    out[-1] *= 0.5
    return out


WK = {n: tables_of(n - 1) for n in (8, 4, 2)}
UP = {(4, 8): interpolation(7, 3), (2, 4): interpolation(3, 1)}
DOWN = {(8, 4): shared(UP[4, 8]).T, (4, 2): shared(UP[2, 4]).T}


def column_blocks(table):
    blocks = np.zeros((table.shape[1], 8))
    blocks[:, : table.shape[0]] = table.T
    return blocks


def constant_table():
    blocks, where = [], {}

    def put(name, rows):
        where[name] = sum(len(b) for b in blocks)
        blocks.append(rows)

    for n in (8, 4, 2):
        w, k = WK[n]
        put(("k", n), column_blocks(k))
        put(("w", n), column_blocks(np.outer(w, w)))
        put(("d", n), column_blocks(np.diag(k)[:, None]))
    for key, table in list(UP.items()) + list(DOWN.items()):
        put(("j",) + key, column_blocks(table))
    flat = np.concatenate(blocks).reshape(-1, 1).astype(np.float32)
    return np.broadcast_to(flat, (flat.shape[0], LANES)).copy(), where


CONST, WHERE = constant_table()


def line(table, values):
    rows, cols = table.shape
    half = cols // 2
    even = [values[k] + values[cols - 1 - k] for k in range(half)]
    odd = [values[k] - values[cols - 1 - k] for k in range(half)]
    out = [None] * rows
    for i in range(rows // 2):
        e = o = None
        for k in range(half):
            te = float(np.float32(0.5 * (table[i, k] + table[i, cols - 1 - k])))
            to = float(np.float32(0.5 * (table[i, k] - table[i, cols - 1 - k])))
            e = te * even[k] if e is None else e + te * even[k]
            o = to * odd[k] if o is None else o + to * odd[k]
        out[i] = e + o
        out[rows - 1 - i] = e - o
    return out


def rows8(start):
    if isinstance(start, int):
        return pl.ds(start, 8)
    return pl.ds(pl.multiple_of(start, 8), 8)


def roll(value, shift):
    shift = shift % LANES
    return value if shift == 0 else pltpu.roll(value, shift, 1)


def loop(count, body, unroll_all):
    if unroll_all:
        for i in range(count):
            body(i)
    else:
        pl.loop(0, count)(body)


def split(i, size):
    if isinstance(i, int):
        return i // size, i % size
    return lax.div(i, size), lax.rem(i, size)


def kernel(
    nz, nr, rhs, stretch, tab, out,
    x7, d7, r7, inv7, o7, t1, t2, x3, d3, r3, inv3, o3, t3, x1, r1, p1, s1, o1, coef,
    send, recv, send_diag, recv_diag, row_box, gz_box, gz_part,
    send_sem, recv_sem, row_send, row_recv, gz_send, gz_recv,
):
    gz = lax.axis_index("gz")
    row = lax.axis_index("row")
    mesh_ids = pl.DeviceIdType.MESH
    shape = (8, LANES)
    lane = lax.broadcasted_iota(jnp.int32, shape, 1)
    sub = lax.broadcasted_iota(jnp.int32, shape, 0)
    in_r = lane % ER
    in_a = (lane // ER) % EA
    low_half = lane < 64

    def as_float(cond):
        return jnp.where(cond, 1.0, 0.0).astype(jnp.float32)

    def at_device(dz, da):
        return (lax.rem(gz + (dz + nz), nz), lax.rem(row + (da + nr), nr))

    barrier = pltpu.get_barrier_semaphore()

    @pl.loop(1, nr)
    def _(o):
        pl.semaphore_signal(barrier, inc=1, device_id=(gz, lax.rem(row + o, nr)), device_id_type=mesh_ids)

    @pl.loop(1, nz)
    def _(o):
        pl.semaphore_signal(barrier, inc=1, device_id=(lax.rem(gz + o, nz), row), device_id_type=mesh_ids)

    for dz, da in DIRS[4:]:
        pl.semaphore_signal(barrier, inc=1, device_id=at_device(dz, da), device_id_type=mesh_ids)

    def const(name, j=0):
        return tab[rows8((WHERE[name] + j) * 8), :]

    def live(n):
        wall = ((sub == 0) & (in_r == 0)) | ((sub == n - 1) & (in_r == ER - 1))
        return jnp.logical_not(wall) & (sub < n)

    for g in range(2):
        for k in range(3):
            coef[rows8((g * 3 + k) * 8), :] = jnp.broadcast_to(
                stretch[pl.ds(k, 1), pl.ds(g * LANES, LANES)], shape
            )

    def coeff(g, k):
        return coef[rows8((g * 3 + k) * 8), :]

    def add_r(field, n, base):
        lo_at = pl.ds(base, 8, stride=8)
        hi_at = pl.ds(base + n - 1, 8, stride=8)
        lo, hi = field[lo_at, :], field[hi_at, :]
        field[lo_at, :] = lo + jnp.where(in_r > 0, roll(hi, 1), 0.0)
        field[hi_at, :] = hi + jnp.where(in_r < ER - 1, roll(lo, -1), 0.0)

    def add_a(field, n, base):
        lo_at, hi_at = rows8(base), rows8(base + (n - 1) * 8)
        lo, hi = field[lo_at, :], field[hi_at, :]
        field[lo_at, :] = lo + jnp.where(in_a > 0, roll(hi, ER), 0.0)
        field[hi_at, :] = hi + jnp.where(in_a < EA - 1, roll(lo, -ER), 0.0)

    def block_at(n, g, iz, ia):
        return rows8(((g * n + iz) * n + ia) * 8)

    def add_z(field, n):
        for ia in range(n):
            at = [block_at(n, g, iz, ia) for g, iz in ((0, 0), (1, 0), (0, n - 1), (1, n - 1))]
            lo0, lo1, hi0, hi1 = [field[a, :] for a in at]
            up0, up1, dn0, dn1 = [roll(v, 64) for v in (hi0, hi1, lo0, lo1)]
            field[at[0], :] = lo0 + jnp.where(low_half, 0.0, up0)
            field[at[1], :] = lo1 + jnp.where(low_half, up0, up1)
            field[at[2], :] = hi0 + jnp.where(low_half, dn0, dn1)
            field[at[3], :] = hi1 + jnp.where(low_half, dn1, 0.0)

    def device_sum(field, n):
        loop(2 * n * n // 8, lambda i: add_r(field, n, i * 64), n < 8)
        loop(2 * n, lambda i: add_a(field, n, i * n * 8), n < 8)
        add_z(field, n)

    def element(field, image, n, sums):
        w, k = WK[n]

        def along_z(i):
            g, ia = split(i, n)
            base = g * (n * n * 8) + ia * 8
            got = line(k, [field[rows8(base + iz * n * 8), :] for iz in range(n)])
            c0 = coef[rows8(g * 24), :]
            for iz in range(n):
                image[rows8(base + iz * n * 8), :] = c0 * got[iz]

        def along_rest(i):
            g, iz = split(i, n)
            base = i * (n * 8)
            got = line(k, [field[rows8(base + ia * 8), :] for ia in range(n)])
            c1 = coef[rows8(g * 24 + 8), :]
            c2 = coef[rows8(g * 24 + 16), :]
            scale = tab[rows8((WHERE["w", n] + iz) * 8), :]
            for ia in range(n):
                at = base + ia * 8
                part = None
                for j in range(n):
                    term = const(("k", n), j) * field[pl.ds(at + j, 1), :]
                    part = term if part is None else part + term
                image[rows8(at), :] = (float(w[ia]) * scale) * (image[rows8(at), :] + c1 * got[ia] + c2 * part)
            if sums and n == 8:
                add_r(image, n, base)
                add_a(image, n, base)

        loop(2 * n, along_z, n < 8)
        loop(2 * n, along_rest, n < 8)
        if sums:
            if n == 8:
                add_z(image, n)
            else:
                device_sum(image, n)

    def diagonal(field, n):
        w, k = WK[n]

        def body(i):
            g, iz = split(i, n)
            c0 = coef[rows8(g * 24), :]
            c1 = coef[rows8(g * 24 + 8), :]
            c2 = coef[rows8(g * 24 + 16), :]
            scale = tab[rows8((WHERE["w", n] + iz) * 8), :]
            kz = jnp.broadcast_to(tab[pl.ds(WHERE["d", n] * 8 + iz, 1), :], shape)
            fixed = c0 * kz + c2 * const(("d", n))
            for ia in range(n):
                field[rows8(i * (n * 8) + ia * 8), :] = (float(w[ia]) * scale) * (fixed + float(k[ia, ia]) * c1)

        loop(2 * n, body, n < 8)

    quarter = in_a

    def pack(field, n, at, at_diag):
        half = n // 2
        for m in range(half):
            rows = rows8(at + m * 8)
            to_up = to_down = None
            for k in range(4):
                g, iz = divmod(m + k * half, n)
                up = roll(field[block_at(n, g, iz, n - 1), :], 80 + 16 * k)
                down = roll(field[block_at(n, g, iz, 0), :], 16 * k)
                to_up = up if k == 0 else jnp.where(quarter == k, up, to_up)
                to_down = down if k == 0 else jnp.where(quarter == k, down, to_down)
            send[0, rows, :] = to_up
            send[1, rows, :] = to_down
            hi = [field[block_at(n, 1, n - 1, ia), :] for ia in (m, m + half)]
            lo = [field[block_at(n, 0, 0, ia), :] for ia in (m, m + half)]
            send[2, rows, :] = jnp.where(low_half, roll(hi[0], 64), hi[1])
            send[3, rows, :] = jnp.where(low_half, lo[0], roll(lo[1], 64))
        rows = rows8(at_diag)
        send_diag[0, rows, :] = field[block_at(n, 1, n - 1, n - 1), :]
        send_diag[1, rows, :] = field[block_at(n, 1, n - 1, 0), :]
        send_diag[2, rows, :] = field[block_at(n, 0, 0, n - 1), :]
        send_diag[3, rows, :] = field[block_at(n, 0, 0, 0), :]

    def unpack(field, n, at, at_diag):
        half = n // 2

        def add(where, keep, value):
            field[where, :] = field[where, :] + jnp.where(keep, value, 0.0)

        for m in range(half):
            rows = rows8(at + m * 8)
            got = [recv[d, rows, :] for d in range(4)]
            for k in range(4):
                g, iz = divmod(m + k * half, n)
                add(block_at(n, g, iz, 0), in_a == 0, roll(got[0], -16 * k))
                add(block_at(n, g, iz, n - 1), in_a == EA - 1, roll(got[1], 48 - 16 * k))
        for m in range(half):
            rows = rows8(at + m * 8)
            got = [recv[d, rows, :] for d in range(4)]
            for k in range(2):
                add(block_at(n, 0, 0, m + k * half), low_half, roll(got[2], 64 * k))
                add(block_at(n, 1, n - 1, m + k * half), jnp.logical_not(low_half), roll(got[3], 64 - 64 * k))
        rows = rows8(at_diag)
        add(block_at(n, 0, 0, 0), lane < 16, roll(recv_diag[0, rows, :], 16))
        add(block_at(n, 0, 0, n - 1), (lane >= 48) & (lane < 64), roll(recv_diag[1, rows, :], -16))
        add(block_at(n, 1, n - 1, 0), (lane >= 64) & (lane < 80), roll(recv_diag[2, rows, :], 16))
        add(block_at(n, 1, n - 1, n - 1), lane >= 112, roll(recv_diag[3, rows, :], -16))

    offsets, diag_offsets = [0], [0]
    for counts in ROUNDS:
        offsets.append(offsets[-1] + sum(counts) * 4)
        diag_offsets.append(diag_offsets[-1] + len(counts) * 8)
    state = {"next": 0}

    def exchange_start(*fields):
        turn = state["next"]
        state["next"] += 1
        counts = ROUNDS[turn]
        at, at_diag = offsets[turn], diag_offsets[turn]
        for field, n in zip(fields, counts):
            pack(field, n, at, at_diag)
            at += n * 4
            at_diag += 8
        copies = []
        for d, (dz, da) in enumerate(DIRS):
            if d < 4:
                rows = pl.ds(offsets[turn], sum(counts) * 4)
                src, dst = send.at[d, rows], recv.at[d, rows]
            else:
                rows = pl.ds(diag_offsets[turn], len(counts) * 8)
                src, dst = send_diag.at[d - 4, rows], recv_diag.at[d - 4, rows]
            copy = pltpu.make_async_remote_copy(
                src_ref=src, dst_ref=dst, send_sem=send_sem.at[turn, d], recv_sem=recv_sem.at[turn, d],
                device_id=at_device(dz, da), device_id_type=mesh_ids,
            )
            copy.start()
            copies.append(copy)

        def finish():
            for copy in copies:
                copy.wait()
            at, at_diag = offsets[turn], diag_offsets[turn]
            for field, n in zip(fields, counts):
                unpack(field, n, at, at_diag)
                at += n * 4
                at_diag += 8

        return finish

    def exchange(*fields):
        exchange_start(*fields)()

    def apply(field, image, n):
        element(field, image, n, True)
        exchange(image)

    def blocks(n, body):
        def step(i):
            if isinstance(i, int):
                body(pl.ds(i * 64, 64))
            else:
                body(pl.ds(pl.multiple_of(i * 64, 64), 64))

        loop(2 * n * n // 8, step, n < 8)

    def masked(n, value):
        keep = jnp.concatenate([as_float(live(n))] * 8, axis=0)
        return keep * value

    @pl.loop(0, 8)
    def _(i):
        rows = pl.ds(pl.multiple_of(i * 64, 64), 64)
        for g in range(2):
            r7[pl.ds(pl.multiple_of(g * 512 + i * 64, 64), 64), :] = rhs[rows, pl.ds(g * LANES, LANES)]

    device_sum(r7, 8)
    diagonal(inv7, 8)
    device_sum(inv7, 8)
    diagonal(inv3, 4)
    device_sum(inv3, 4)
    pl.semaphore_wait(barrier, (nr - 1) + (nz - 1) + 4)
    exchange(r7, inv7, inv3)

    def invert(inv, n):
        keep = jnp.concatenate([live(n)] * 8, axis=0)

        def body(at):
            inv[at, :] = jnp.where(keep, 1.0 / jnp.where(keep, inv[at, :], 1.0), 0.0)

        blocks(n, body)

    invert(inv7, 8)
    invert(inv3, 4)

    def smooth_first(inv, r, d, n):
        def body(at):
            d[at, :] = (1.0 / THETA) * (inv[at, :] * r[at, :])

        blocks(n, body)

    def smooth_second(inv, r, d, x, image, n, add, keep_r=True):
        def body(at):
            step = d[at, :]
            left = r[at, :] - image[at, :]
            second = (RHO2 * RHO) * step + (2.0 * RHO2 / DELTA) * (inv[at, :] * left)
            x[at, :] = (x[at, :] + (step + second)) if add else step + second
            if keep_r:
                d[at, :] = second
                r[at, :] = left

        blocks(n, body)

    def residual(r, image, n):
        def body(at):
            r[at, :] = masked(n, r[at, :] - image[at, :])

        blocks(n, body)

    def r_line(name, field, at, count):
        part = None
        for j in range(count):
            term = const(name, j) * field[pl.ds(at + j, 1), :]
            part = term if part is None else part + term
        return part

    def restrict(fine, nf, nc, coarse, tz, ta):
        table = DOWN[nf, nc]

        def along_z(i):
            g, ia = split(i, nf)
            got = line(table, [fine[rows8((g * nf + iz) * (nf * 8) + ia * 8), :] for iz in range(nf)])
            for c in range(nc):
                tz[rows8((g * nc + c) * (nf * 8) + ia * 8), :] = got[c]

        def along_a(i):
            got = line(table, [tz[rows8(i * (nf * 8) + ia * 8), :] for ia in range(nf)])
            for c in range(nc):
                ta[rows8(i * (nc * 8) + c * 8), :] = got[c]
            for c in range(nc):
                at = i * (nc * 8) + c * 8
                coarse[rows8(at), :] = r_line(("j", nf, nc), ta, at, nf)

        loop(2 * nf, along_z, nf < 8)
        loop(2 * nc, along_a, nf < 8)

    def prolong(coarse, nc, nf, fine, tz, ta):
        table = UP[nc, nf]

        def along_a(i):
            for c in range(nc):
                at = i * (nc * 8) + c * 8
                ta[rows8(at), :] = r_line(("j", nc, nf), coarse, at, nc)
            got = line(table, [ta[rows8(i * (nc * 8) + c * 8), :] for c in range(nc)])
            for ia in range(nf):
                tz[rows8(i * (nf * 8) + ia * 8), :] = got[ia]

        def along_z(i):
            g, ia = split(i, nf)
            got = line(table, [tz[rows8((g * nc + c) * (nf * 8) + ia * 8), :] for c in range(nc)])
            for iz in range(nf):
                fine[rows8((g * nf + iz) * (nf * 8) + ia * 8), :] = got[iz]

        loop(2 * nc, along_a, nf < 8)
        loop(2 * nf, along_z, nf < 8)

    smooth_first(inv7, r7, d7, 8)
    apply(d7, o7, 8)
    smooth_second(inv7, r7, d7, x7, o7, 8, False)
    apply(d7, o7, 8)
    residual(r7, o7, 8)

    restrict(r7, 8, 4, r3, t1, t2)
    device_sum(r3, 4)
    exchange(r3)
    smooth_first(inv3, r3, d3, 4)
    apply(d3, o3, 4)
    smooth_second(inv3, r3, d3, x3, o3, 4, False)
    apply(d3, o3, 4)
    residual(r3, o3, 4)

    restrict(r3, 4, 2, r1, t3, t2)
    device_sum(r1, 2)
    exchange(r1)
    r1[...] = masked(2, r1[...])

    def all_sum_start(turn, first, second):
        def column(value):
            total = value[0:8]
            for k in range(1, 8):
                total = total + value[k * 8 : k * 8 + 8]
            return jnp.sum(total, axis=0, keepdims=True)

        row_box[turn, 0, pl.ds(0, 1), :] = column(first)
        row_box[turn, 0, pl.ds(1, 1), :] = column(second)

        @pl.loop(1, nr)
        def _(o):
            pltpu.make_async_remote_copy(
                src_ref=row_box.at[turn, 0], dst_ref=row_box.at[turn, o],
                send_sem=row_send.at[turn], recv_sem=row_recv.at[turn],
                device_id=(gz, lax.rem(row + o, nr)), device_id_type=mesh_ids,
            ).start()

    def wait_for(box, turn, count, sem):
        rest = box.at[turn, pl.ds(1, count - 1)]
        pltpu.make_async_copy(rest, rest, sem.at[turn]).wait()

    def total_of(box, turn, count):
        total = box[turn, 0]
        for o in range(1, count):
            total = total + box[turn, o]
        return total

    def all_sum_middle(turn):
        wait_for(row_box, turn, nr, row_recv)
        gz_box[turn, 0] = total_of(row_box, turn, nr)

        @pl.loop(1, nz)
        def _(o):
            pltpu.make_async_remote_copy(
                src_ref=gz_box.at[turn, 0], dst_ref=gz_box.at[turn, o],
                send_sem=gz_send.at[turn], recv_sem=gz_recv.at[turn],
                device_id=(lax.rem(gz + o, nz), row), device_id_type=mesh_ids,
            ).start()

    def all_sum_finish(turn):
        wait_for(gz_box, turn, nz, gz_recv)
        gz_part[...] = total_of(gz_box, turn, nz)
        total = jnp.sum(gz_part[...], axis=1, keepdims=True)
        wait_for(row_box, turn, nr, row_send)
        wait_for(gz_box, turn, nz, gz_send)
        return total[0:1, :], total[1:2, :]

    norm_old = alpha = None
    for turn in range(ITERS):
        last = turn == ITERS - 1
        element(r1, o1, 2, False)
        res = r1[...]
        all_sum_start(turn, 0.125 * (res * res), res * o1[...])
        finish = None
        if not last:
            device_sum(o1, 2)
            finish = exchange_start(o1)
        all_sum_middle(turn)
        if not last:
            finish()
        norm, energy = all_sum_finish(turn)
        if turn == 0:
            alpha = norm / energy
            direction = res
        else:
            beta = norm / norm_old
            alpha = norm / (energy - beta * norm / alpha)
            direction = res + beta * p1[...]
        norm_old = norm
        x1[...] = alpha * direction if turn == 0 else x1[...] + alpha * direction
        if not last:
            image = masked(2, o1[...])
            if turn > 0:
                image = image + beta * s1[...]
            p1[...] = direction
            s1[...] = image
            r1[...] = res - alpha * image

    prolong(x1, 2, 4, d3, t3, t2)
    x3[...] = x3[...] + d3[...]
    apply(d3, o3, 4)
    r3[...] = r3[...] - o3[...]
    smooth_first(inv3, r3, d3, 4)
    apply(d3, o3, 4)
    smooth_second(inv3, r3, d3, x3, o3, 4, True, False)

    prolong(x3, 4, 8, d7, t1, t2)
    apply(d7, o7, 8)

    def before_last(at):
        x7[at, :] = x7[at, :] + d7[at, :]
        left = r7[at, :] - o7[at, :]
        r7[at, :] = left
        d7[at, :] = (1.0 / THETA) * (inv7[at, :] * left)

    blocks(8, before_last)
    apply(d7, o7, 8)
    smooth_second(inv7, r7, d7, x7, o7, 8, True, False)

    @pl.loop(0, 8)
    def _(i):
        rows = pl.ds(pl.multiple_of(i * 64, 64), 64)
        for g in range(2):
            out[rows, pl.ds(g * LANES, LANES)] = x7[pl.ds(pl.multiple_of(g * 512 + i * 64, 64), 64), :]


def per_device(rhs_local, stretch):
    nz = lax.axis_size("gz")
    nr = lax.axis_size("row")
    nodes = (ORDER + 1) ** 3
    elems = EZ * EA * ER
    face_rows = sum(sum(c) * 4 for c in ROUNDS)
    diag_rows = sum(len(c) * 8 for c in ROUNDS)

    def field(rows):
        return pltpu.VMEM((rows, LANES), jnp.float32)

    out = pl.pallas_call(
        functools.partial(kernel, nz, nr),
        out_shape=jax.ShapeDtypeStruct((nodes, elems), jnp.float32),
        in_specs=[pl.BlockSpec(memory_space=pltpu.VMEM)] * 3,
        out_specs=pl.BlockSpec(memory_space=pltpu.VMEM),
        scratch_shapes=[field(1024)] * 5
        + [field(512), field(256)]
        + [field(256)] * 5
        + [field(128)]
        + [field(64)] * 5
        + [field(48)]
        + [
            pltpu.VMEM((4, face_rows, LANES), jnp.float32),
            pltpu.VMEM((4, face_rows, LANES), jnp.float32),
            pltpu.VMEM((4, diag_rows, LANES), jnp.float32),
            pltpu.VMEM((4, diag_rows, LANES), jnp.float32),
            pltpu.VMEM((ITERS, nr, 2, LANES), jnp.float32),
            pltpu.VMEM((ITERS, nz, 2, LANES), jnp.float32),
            pltpu.VMEM((2, LANES), jnp.float32),
            pltpu.SemaphoreType.DMA((len(ROUNDS), 8)),
            pltpu.SemaphoreType.DMA((len(ROUNDS), 8)),
            pltpu.SemaphoreType.DMA((ITERS,)),
            pltpu.SemaphoreType.DMA((ITERS,)),
            pltpu.SemaphoreType.DMA((ITERS,)),
            pltpu.SemaphoreType.DMA((ITERS,)),
        ],
        compiler_params=pltpu.CompilerParams(
            collective_id=0, has_side_effects=True, vmem_limit_bytes=32 * 1024 * 1024
        ),
    )(rhs_local.reshape(nodes, elems), stretch, jnp.asarray(CONST))
    return out.reshape(rhs_local.shape)


def solution(mesh):
    placed = (P(None, None, None, ("gz", "row")), P(None, ("gz", "row")))
    return jax.shard_map(
        per_device,
        mesh=mesh,
        in_specs=placed,
        out_specs=P(None, None, None, ("gz", "row")),
        check_vma=False,
    )
```

time: 1470 us -> 156 us (0.11); the launches traced: 1450 us -> 156 us
  blocking collectives: 923 us -> 0 us
  starting transfers between devices: 271 us -> 0 us
  Pallas kernels: 0 us -> 153 us
  local copies, waits for them, and re-layouts: 125 us -> 3.45 us
  waiting for transfers between devices: 40.9 us -> 0 us
  other arithmetic: 38.8 us -> 0 us
  between operations: 33.2 us -> 0.01 us
  matrix products: 21.9 us -> 0 us
    psum x9 -> x0, blocking collectives: 923 us -> none  [the longest x5 506 us: squared_norm(): return lax.psum(jnp.sum(weight * values * values), ('gz', 'row'))]
    ppermute x72 -> x0, starting transfers between devices: 271 us -> none  [the longest x36 183 us: with_halo(): lax.ppermute(head, axis, [((i + 1) % count, i) for i in range(count)])]
    pallas_call x0 -> x1, Pallas kernels: none -> 153 us  [per_device(): pl.pallas_call(functools.partial(kernel, nz, nr), out_shape=jax.ShapeDtyp...]
    ppermute x72 -> x0, waiting for transfers between devices: 40.9 us -> none  [the longest x36 21.4 us: with_halo(): lax.ppermute(tail, axis, [(i, (i + 1) % count) for i in range(count)])]
    scatter x77 -> x0, local copies, waits for them, and re-layouts: 27.2 us -> none  [the longest x37 15.6 us: face_add(): moved = moved.at[size - 1].set(high_face + from_above)]
    slice x147 -> x0, local copies, waits for them, and re-layouts: 27.1 us -> none  [the longest x36 7.99 us: face_add(): high_edge = high_face.reshape(split_shape)[..., count - 1, :]]
    dot_general x54 -> x0, matrix products: 21.9 us -> none  [the longest x13 6.6 us: element_apply(): jnp.einsum('ij,jbc...->ibc...', stiffness, field, precision=HIGHEST)]
    broadcast_in_dim x108 -> x0, local copies, waits for them, and re-layouts: 17.6 us -> none  [the longest x54 8.79 us: face_add(): jnp.broadcast_to(padded[0][..., None, :], split_shape)]
  transfers between devices with their start and end apart: 72 -> 0, of which waited for: 21 -> 0; matrix products, arithmetic and copies ran while one was open for 5% -> 0% of each run, Pallas kernels for 0% -> 0%
where the time goes in v1:
time: 156 us
  Pallas kernels  153 us (98%)
  local copies, waits for them, and re-layouts  3.45 us (2%)
    pallas_call x1, Pallas kernels, per_device(): pl.pallas_call(functools.partial(kernel, nz, nr), out_shape=jax.ShapeDtyp...  153 us
    unnamed x7, local copies, waits for them, and re-layouts  3.45 us

profile of v1, /device:TPU:1, one launch (start us, length us, event | category | flops | bytes accessed | tf_op | source)
XLA Modules:
  0.0 156.3 jit_solution(10501810284491324665)
XLA Ops:
  0.0 0.0 copy-start
  0.0 1.0 copy-done
  1.0 0.0 copy-start.1
  1.0 0.9 copy-done.1
  2.0 0.0 copy-start.2
  2.0 0.7 copy-done.2
  2.7 152.8 %shard_map.37 = f32[512,256]{1,0:T(8,128)S(1)} custom-call(f32[512,256]{1,0:T(8,128)S(1)} %bitcast.3, f32[3,256]{1,0:T(4,128)S(1)} %copy-done.2, f32[392,128]{1,0:T(8,128)S(1)} %copy-done.1), custom_call_target="tpu_custom_call" | custom-call | tf_op jit(solution)/shard_map/pallas_call | solution.py:625
  155.5 0.8 copy.5
Async XLA Ops:
  0.0 1.0 copy-start
  1.0 0.9 copy-start.1
  2.0 0.7 copy-start.2

commit v2 on v1

--- a/solution.py
+++ b/solution.py
@@ -25,7 +25,9 @@
 RHO2 = 1.0 / (2.0 * THETA / DELTA - RHO)
 
 DIRS = ((0, 1), (0, -1), (1, 0), (-1, 0), (1, 1), (1, -1), (-1, 1), (-1, -1))
-ROUNDS = ((8, 8, 4), (8,), (8,), (4,), (4,), (4,), (2,), (2,), (2,), (2,), (2,), (4,), (4,), (8,), (8,))
+ROUNDS = ((8, 8, 4), (8,), (4,), (4,), (2,), (4,), (4,), (8,), (8,))
+SCALE = 16.0
+TINY = 1e-13
 
 
 def points_of(order):
@@ -60,16 +62,10 @@
     return table
 
 
-def shared(table):
-    out = table.copy()
-    out[0] *= 0.5
-    out[-1] *= 0.5
-    return out
-
-
 WK = {n: tables_of(n - 1) for n in (8, 4, 2)}
 UP = {(4, 8): interpolation(7, 3), (2, 4): interpolation(3, 1)}
-DOWN = {(8, 4): shared(UP[4, 8]).T, (4, 2): shared(UP[2, 4]).T}
+DOWN = {(8, 4): UP[4, 8].T, (4, 2): UP[2, 4].T}
+PAIRS = [(i, j) for i in range(ITERS) for j in range(i, ITERS)] + [(i, ITERS) for i in range(ITERS)]
 
 
 def column_blocks(table):
@@ -93,7 +89,14 @@
     for key, table in list(UP.items()) + list(DOWN.items()):
         put(("j",) + key, column_blocks(table))
     flat = np.concatenate(blocks).reshape(-1, 1).astype(np.float32)
-    return np.broadcast_to(flat, (flat.shape[0], LANES)).copy(), where
+    wide = np.broadcast_to(flat, (flat.shape[0], LANES))
+    where["pick"] = wide.shape[0] // 8
+    pick = np.zeros((24, LANES), np.float32)
+    for e, (i, j) in enumerate(PAIRS):
+        pick[e, 8 * i + j] = 1.0
+        if j < ITERS:
+            pick[e, 8 * j + i] = 1.0
+    return np.concatenate([wide, pick]), where
 
 
 CONST, WHERE = constant_table()
@@ -142,11 +145,46 @@
     return lax.div(i, size), lax.rem(i, size)
 
 
+def two_sum(a, b):
+    s = a + b
+    t = s - a
+    return s, (a - (s - t)) + (b - t)
+
+
+def halves(a):
+    t = 4097.0 * a
+    hi = t - (t - a)
+    return a, hi, a - hi
+
+
+def two_prod(x, y):
+    a, ah, al = x
+    b, bh, bl = y
+    p = a * b
+    return p, ((ah * bh - p) + ah * bl + al * bh) + al * bl
+
+
+def add2(x, y):
+    s, e = two_sum(x[0], y[0])
+    return two_sum(s, e + (x[1] + y[1]))
+
+
+def mul2(x, y):
+    p, e = two_prod(halves(x[0]), halves(y[0]))
+    return two_sum(p, e + (x[0] * y[1] + x[1] * y[0]))
+
+
+def inverse2(x):
+    r = 1.0 / x[0]
+    p, e = two_prod(halves(x[0]), halves(r))
+    return two_sum(r, r * (((1.0 - p) - e) - x[1] * r))
+
+
 def kernel(
     nz, nr, rhs, stretch, tab, out,
-    x7, d7, r7, inv7, o7, t1, t2, x3, d3, r3, inv3, o3, t3, x1, r1, p1, s1, o1, coef,
-    send, recv, send_diag, recv_diag, row_box, gz_box, gz_part,
-    send_sem, recv_sem, row_send, row_recv, gz_send, gz_recv,
+    x7, d7, r7, inv7, o7, t1, t2, x3, d3, r3, inv3, o3, t3, x1, r1, coef,
+    send, recv, send_diag, recv_diag, send_block, recv_block, row_box, gz_box,
+    send_sem, recv_sem, block_send, block_recv, row_send, row_recv, gz_send, gz_recv,
 ):
     gz = lax.axis_index("gz")
     row = lax.axis_index("row")
@@ -224,7 +262,15 @@
         loop(2 * n, lambda i: add_a(field, n, i * n * 8), n < 8)
         add_z(field, n)
 
-    def element(field, image, n, sums):
+    def shared(iz, ia, n):
+        along = jnp.where((sub == 0) | (sub == n - 1), 0.5, 1.0)
+        if ia in (0, n - 1):
+            along = 0.5 * along
+        if isinstance(iz, int):
+            return 0.5 * along if iz in (0, n - 1) else along
+        return jnp.where((iz == 0) | (iz == n - 1), 0.5, 1.0) * along
+
+    def element(field, image, n, sums, left=None):
         w, k = WK[n]
 
         def along_z(i):
@@ -248,7 +294,10 @@
                 for j in range(n):
                     term = const(("k", n), j) * field[pl.ds(at + j, 1), :]
                     part = term if part is None else part + term
-                image[rows8(at), :] = (float(w[ia]) * scale) * (image[rows8(at), :] + c1 * got[ia] + c2 * part)
+                value = (float(w[ia]) * scale) * (image[rows8(at), :] + c1 * got[ia] + c2 * part)
+                if left is not None:
+                    value = shared(iz, ia, n) * left[rows8(at), :] - value
+                image[rows8(at), :] = value
             if sums and n == 8:
                 add_r(image, n, base)
                 add_a(image, n, base)
@@ -368,6 +417,34 @@
 
         return finish
 
+    def block_start(turn, at, count):
+        copies = []
+        for d, (dz, da) in enumerate(DIRS):
+            copy = pltpu.make_async_remote_copy(
+                src_ref=send_block.at[pl.ds(at, count)], dst_ref=recv_block.at[d, pl.ds(at, count)],
+                send_sem=block_send.at[turn, d], recv_sem=block_recv.at[turn, d],
+                device_id=at_device(dz, da), device_id_type=mesh_ids,
+            )
+            copy.start()
+            copies.append(copy)
+        return copies
+
+    def wide(at):
+        def block(dz, da):
+            if (dz, da) == (0, 0):
+                return send_block[rows8(at), :]
+            return recv_block[DIRS.index((-dz, -da)), rows8(at), :]
+
+        def left_part(dz):
+            return jnp.where(low_half, block(dz, -1), roll(block(dz, 0), 64))
+
+        def below(low, own):
+            return jnp.where(sub < 4, low, pltpu.roll(own, 4, 0))
+
+        top = jnp.concatenate([below(left_part(-1), left_part(0)), below(block(-1, 1), block(0, 1))], axis=1)
+        bottom = jnp.concatenate([left_part(1), block(1, 1)], axis=1)
+        return jnp.concatenate([top, bottom], axis=0)
+
     def exchange(*fields):
         exchange_start(*fields)()
 
@@ -399,8 +476,13 @@
     device_sum(inv7, 8)
     diagonal(inv3, 4)
     device_sum(inv3, 4)
+    for k in range(3):
+        rows = jnp.where(sub < 2, coeff(0, k), coeff(1, k))
+        send_block[rows8(k * 8), :] = jnp.where(sub % 2 == 0, rows, roll(rows, 64))
     pl.semaphore_wait(barrier, (nr - 1) + (nz - 1) + 4)
-    exchange(r7, inv7, inv3)
+    finish_first = exchange_start(r7, inv7, inv3)
+    stretch_copies = block_start(0, 0, 24)
+    finish_first()
 
     def invert(inv, n):
         keep = jnp.concatenate([live(n)] * 8, axis=0)
@@ -431,12 +513,6 @@
 
         blocks(n, body)
 
-    def residual(r, image, n):
-        def body(at):
-            r[at, :] = masked(n, r[at, :] - image[at, :])
-
-        blocks(n, body)
-
     def r_line(name, field, at, count):
         part = None
         for j in range(count):
@@ -464,7 +540,7 @@
         loop(2 * nf, along_z, nf < 8)
         loop(2 * nc, along_a, nf < 8)
 
-    def prolong(coarse, nc, nf, fine, tz, ta):
+    def prolong(coarse, nc, nf, fields, tz, ta):
         table = UP[nc, nf]
 
         def along_a(i):
@@ -479,7 +555,9 @@
             g, ia = split(i, nf)
             got = line(table, [tz[rows8((g * nc + c) * (nf * 8) + ia * 8), :] for c in range(nc)])
             for iz in range(nf):
-                fine[rows8((g * nf + iz) * (nf * 8) + ia * 8), :] = got[iz]
+                at = rows8((g * nf + iz) * (nf * 8) + ia * 8)
+                for field in fields:
+                    field[at, :] = field[at, :] + got[iz]
 
         loop(2 * nc, along_a, nf < 8)
         loop(2 * nf, along_z, nf < 8)
@@ -487,115 +565,185 @@
     smooth_first(inv7, r7, d7, 8)
     apply(d7, o7, 8)
     smooth_second(inv7, r7, d7, x7, o7, 8, False)
-    apply(d7, o7, 8)
-    residual(r7, o7, 8)
-
-    restrict(r7, 8, 4, r3, t1, t2)
+    element(d7, o7, 8, False, left=r7)
+
+    restrict(o7, 8, 4, r3, t1, t2)
     device_sum(r3, 4)
     exchange(r3)
     smooth_first(inv3, r3, d3, 4)
     apply(d3, o3, 4)
     smooth_second(inv3, r3, d3, x3, o3, 4, False)
-    apply(d3, o3, 4)
-    residual(r3, o3, 4)
-
-    restrict(r3, 4, 2, r1, t3, t2)
+    element(d3, o3, 4, False, left=r3)
+
+    restrict(o3, 4, 2, r1, t3, t2)
     device_sum(r1, 2)
     exchange(r1)
     r1[...] = masked(2, r1[...])
 
-    def all_sum_start(turn, first, second):
-        def column(value):
-            total = value[0:8]
-            for k in range(1, 8):
-                total = total + value[k * 8 : k * 8 + 8]
-            return jnp.sum(total, axis=0, keepdims=True)
-
-        row_box[turn, 0, pl.ds(0, 1), :] = column(first)
-        row_box[turn, 0, pl.ds(1, 1), :] = column(second)
-
-        @pl.loop(1, nr)
-        def _(o):
-            pltpu.make_async_remote_copy(
-                src_ref=row_box.at[turn, 0], dst_ref=row_box.at[turn, o],
-                send_sem=row_send.at[turn], recv_sem=row_recv.at[turn],
-                device_id=(gz, lax.rem(row + o, nr)), device_id_type=mesh_ids,
-            ).start()
-
-    def wait_for(box, turn, count, sem):
-        rest = box.at[turn, pl.ds(1, count - 1)]
-        pltpu.make_async_copy(rest, rest, sem.at[turn]).wait()
-
-    def total_of(box, turn, count):
-        total = box[turn, 0]
-        for o in range(1, count):
-            total = total + box[turn, o]
-        return total
-
-    def all_sum_middle(turn):
-        wait_for(row_box, turn, nr, row_recv)
-        gz_box[turn, 0] = total_of(row_box, turn, nr)
-
-        @pl.loop(1, nz)
-        def _(o):
-            pltpu.make_async_remote_copy(
-                src_ref=gz_box.at[turn, 0], dst_ref=gz_box.at[turn, o],
-                send_sem=gz_send.at[turn], recv_sem=gz_recv.at[turn],
-                device_id=(lax.rem(gz + o, nz), row), device_id_type=mesh_ids,
-            ).start()
-
-    def all_sum_finish(turn):
-        wait_for(gz_box, turn, nz, gz_recv)
-        gz_part[...] = total_of(gz_box, turn, nz)
-        total = jnp.sum(gz_part[...], axis=1, keepdims=True)
-        wait_for(row_box, turn, nr, row_send)
-        wait_for(gz_box, turn, nz, gz_send)
-        return total[0:1, :], total[1:2, :]
-
-    norm_old = alpha = None
-    for turn in range(ITERS):
-        last = turn == ITERS - 1
-        element(r1, o1, 2, False)
-        res = r1[...]
-        all_sum_start(turn, 0.125 * (res * res), res * o1[...])
-        finish = None
-        if not last:
-            device_sum(o1, 2)
-            finish = exchange_start(o1)
-        all_sum_middle(turn)
-        if not last:
-            finish()
-        norm, energy = all_sum_finish(turn)
-        if turn == 0:
-            alpha = norm / energy
-            direction = res
+    for copy in stretch_copies:
+        copy.wait()
+    lane_wide = lax.broadcasted_iota(jnp.int32, (16, 256), 1)
+    inside = lane_wide % ER > 0
+
+    def step(value, axis, amount):
+        if axis == 0:
+            return pltpu.roll(value, amount % 16, 0)
+        return pltpu.roll(value, (amount * (ER if axis == 1 else 1)) % 256, 1)
+
+    edges = []
+    for axis in range(3):
+        total = wide(axis * 8)
+        for other in range(3):
+            if other != axis:
+                total = total + step(total, other, 1)
+        edges.append(0.5 * total)
+
+    def differences(value):
+        return [value - step(value, axis, -1) for axis in range(3)]
+
+    def vertex_image(slopes):
+        total = None
+        for axis in range(3):
+            flux = edges[axis] * slopes[axis]
+            flux = flux - step(flux, axis, 1)
+            total = flux if total is None else total + flux
+        return jnp.where(inside, (1.0 / SCALE) * total, 0.0)
+
+    def vertex_row(g, iz, odd):
+        inner = jnp.broadcast_to(r1[pl.ds(((g * 2 + iz) * 2) * 8, 1), :], shape)
+        outer = jnp.broadcast_to(r1[pl.ds(((g * 2 + iz) * 2 + 1) * 8, 1), :], shape)
+        shift = 64 if odd else 0
+        return jnp.where(low_half, roll(inner, shift), roll(outer, shift + ER))
+
+    block = vertex_row(1, 1, True)
+    for z in range(EZ):
+        block = jnp.where(sub == z, vertex_row(z // 2, 0, z % 2 == 1), block)
+    send_block[rows8(24), :] = block
+    for copy in block_start(1, 24, 8):
+        copy.wait()
+
+    basis = [wide(24)]
+    slopes = [differences(basis[0])]
+    for k in range(1, ITERS):
+        basis.append(vertex_image(slopes[-1]))
+        slopes.append(differences(basis[-1]))
+
+    own = (sub >= 4) & jnp.logical_not(low_half)
+    roots = [jnp.where(own, jnp.sqrt(edge[0:8, 0:LANES]), 0.0) for edge in edges]
+    flows = [[halves(roots[axis] * slope[axis][0:8, 0:LANES]) for axis in range(3)] for slope in slopes]
+    points = [halves(jnp.where(own, value[0:8, 0:LANES], 0.0)) for value in basis]
+
+    tiles = [None] * 6
+    for e, (i, j) in enumerate(PAIRS):
+        if j < ITERS:
+            total = two_prod(flows[i][0], flows[j][0])
+            for axis in (1, 2):
+                total = add2(total, two_prod(flows[i][axis], flows[j][axis]))
         else:
-            beta = norm / norm_old
-            alpha = norm / (energy - beta * norm / alpha)
-            direction = res + beta * p1[...]
-        norm_old = norm
-        x1[...] = alpha * direction if turn == 0 else x1[...] + alpha * direction
-        if not last:
-            image = masked(2, o1[...])
-            if turn > 0:
-                image = image + beta * s1[...]
-            p1[...] = direction
-            s1[...] = image
-            r1[...] = res - alpha * image
-
-    prolong(x1, 2, 4, d3, t3, t2)
-    x3[...] = x3[...] + d3[...]
+            total = two_prod(points[i], points[0])
+        for amount in (2, 1):
+            total = add2(total, tuple(pltpu.roll(part, amount, 0) for part in total))
+        for half in range(2):
+            row_of = jnp.broadcast_to(total[half][7:8, :], shape)
+            slot = 2 * (e // 8) + half
+            tiles[slot] = row_of if e % 8 == 0 else jnp.where(sub == e % 8, row_of, tiles[slot])
+    sent = [0.0, 0.0]
+    for t in range(3):
+        total = (tiles[2 * t], tiles[2 * t + 1])
+        for amount in (64, 32, 16, 8, 4, 2, 1):
+            total = add2(total, tuple(roll(part, amount) for part in total))
+        pick = tab[rows8((WHERE["pick"] + t) * 8), :] > 0.0
+        for half in range(2):
+            sent[half] = sent[half] + jnp.sum(jnp.where(pick, total[half], 0.0), axis=0, keepdims=True)
+    for half in range(2):
+        row_box[0, pl.ds(half, 1), :] = sent[half]
+
+    @pl.loop(1, nr)
+    def _(o):
+        pltpu.make_async_remote_copy(
+            src_ref=row_box.at[0], dst_ref=row_box.at[o], send_sem=row_send, recv_sem=row_recv,
+            device_id=(gz, lax.rem(row + o, nr)), device_id_type=mesh_ids,
+        ).start()
+
+    def wait_for(box, count, sem):
+        rest = box.at[pl.ds(1, count - 1)]
+        pltpu.make_async_copy(rest, rest, sem).wait()
+
+    def total_of(box, count):
+        parts = [(box[o, pl.ds(0, 1), :], box[o, pl.ds(1, 1), :]) for o in range(count)]
+        while len(parts) > 1:
+            half = len(parts) // 2
+            parts = [add2(parts[k], parts[k + half]) for k in range(half)] + parts[2 * half :]
+        return parts[0]
+
+    wait_for(row_box, nr, row_recv)
+    total = total_of(row_box, nr)
+    for half in range(2):
+        gz_box[0, pl.ds(half, 1), :] = total[half]
+
+    @pl.loop(1, nz)
+    def _(o):
+        pltpu.make_async_remote_copy(
+            src_ref=gz_box.at[0], dst_ref=gz_box.at[o], send_sem=gz_send, recv_sem=gz_recv,
+            device_id=(lax.rem(gz + o, nz), row), device_id_type=mesh_ids,
+        ).start()
+
+    wait_for(gz_box, nz, gz_recv)
+    total = total_of(gz_box, nz)
+    wait_for(row_box, nr, row_send)
+    wait_for(gz_box, nz, gz_send)
+
+    system = []
+    for half in range(2):
+        wide_row = jnp.broadcast_to(total[half], shape)
+        part = jnp.zeros(shape, jnp.float32)
+        for i in range(ITERS):
+            part = jnp.where(sub == i, roll(wide_row, -8 * i), part)
+        system.append(jnp.where(lane <= ITERS, part, 0.0))
+    start = system[0]
+    for p in range(ITERS):
+        column = [jnp.broadcast_to(part[:, p : p + 1], shape) for part in system]
+        line_p = [jnp.broadcast_to(part[p : p + 1, :], shape) for part in system]
+        pivot = [jnp.broadcast_to(part[p : p + 1, :], shape) for part in column]
+        least = TINY * jnp.broadcast_to(jnp.broadcast_to(start[p : p + 1, :], shape)[:, p : p + 1], shape)
+        usable = pivot[0] > least
+        inverse = inverse2((jnp.where(usable, pivot[0], 1.0), jnp.where(usable, pivot[1], 0.0)))
+        scaled = mul2(line_p, tuple(jnp.where(usable, part, 0.0) for part in inverse))
+        taken = mul2(column, scaled)
+        rest = add2(system, (-taken[0], -taken[1]))
+        system = [jnp.where(sub == p, scaled[half], rest[half]) for half in range(2)]
+
+    solved = None
+    for k in range(ITERS):
+        factor = jnp.broadcast_to(jnp.broadcast_to(system[0][k : k + 1, :], (16, LANES))[:, ITERS : ITERS + 1], (16, 256))
+        term = factor * basis[k]
+        solved = term if solved is None else solved + term
+
+    for ia in range(2):
+        at_node = []
+        for ir in range(2):
+            back = 64 + ER * ia + ir
+            at_node.append([pltpu.roll(solved, (shift - back) % 256, 1)[:, 0:LANES] for shift in (0, 64)])
+        for g in range(2):
+            for iz in range(2):
+                row_at = 4 + 2 * g + iz
+                pair = [
+                    jnp.where(low_half, jnp.broadcast_to(v[0][row_at : row_at + 1], shape), jnp.broadcast_to(v[1][row_at + 1 : row_at + 2], shape))
+                    for v in at_node
+                ]
+                x1[block_at(2, g, iz, ia), :] = jnp.where(sub == 0, pair[0], jnp.where(sub == 1, pair[1], 0.0))
+
+    prolong(x1, 2, 4, (d3, x3), t3, t2)
     apply(d3, o3, 4)
     r3[...] = r3[...] - o3[...]
     smooth_first(inv3, r3, d3, 4)
     apply(d3, o3, 4)
     smooth_second(inv3, r3, d3, x3, o3, 4, True, False)
 
-    prolong(x3, 4, 8, d7, t1, t2)
+    prolong(x3, 4, 8, (d7, x7), t1, t2)
     apply(d7, o7, 8)
 
     def before_last(at):
-        x7[at, :] = x7[at, :] + d7[at, :]
         left = r7[at, :] - o7[at, :]
         r7[at, :] = left
         d7[at, :] = (1.0 / THETA) * (inv7[at, :] * left)
@@ -631,22 +779,25 @@
         + [field(512), field(256)]
         + [field(256)] * 5
         + [field(128)]
-        + [field(64)] * 5
+        + [field(64)] * 2
         + [field(48)]
         + [
             pltpu.VMEM((4, face_rows, LANES), jnp.float32),
             pltpu.VMEM((4, face_rows, LANES), jnp.float32),
             pltpu.VMEM((4, diag_rows, LANES), jnp.float32),
             pltpu.VMEM((4, diag_rows, LANES), jnp.float32),
-            pltpu.VMEM((ITERS, nr, 2, LANES), jnp.float32),
-            pltpu.VMEM((ITERS, nz, 2, LANES), jnp.float32),
-            pltpu.VMEM((2, LANES), jnp.float32),
+            pltpu.VMEM((32, LANES), jnp.float32),
+            pltpu.VMEM((8, 32, LANES), jnp.float32),
+            pltpu.VMEM((nr, 2, LANES), jnp.float32),
+            pltpu.VMEM((nz, 2, LANES), jnp.float32),
             pltpu.SemaphoreType.DMA((len(ROUNDS), 8)),
             pltpu.SemaphoreType.DMA((len(ROUNDS), 8)),
-            pltpu.SemaphoreType.DMA((ITERS,)),
-            pltpu.SemaphoreType.DMA((ITERS,)),
-            pltpu.SemaphoreType.DMA((ITERS,)),
-            pltpu.SemaphoreType.DMA((ITERS,)),
+            pltpu.SemaphoreType.DMA((2, 8)),
+            pltpu.SemaphoreType.DMA((2, 8)),
+            pltpu.SemaphoreType.DMA,
+            pltpu.SemaphoreType.DMA,
+            pltpu.SemaphoreType.DMA,
+            pltpu.SemaphoreType.DMA,
         ],
         compiler_params=pltpu.CompilerParams(
             collective_id=0, has_side_effects=True, vmem_limit_bytes=32 * 1024 * 1024

time: 156 us -> 102 us (0.65)
  Pallas kernels: 153 us -> 97.9 us
    pallas_call x1, Pallas kernels: 153 us -> 97.9 us  [per_device(): pl.pallas_call(functools.partial(kernel, nz, nr), out_shape=jax.ShapeDtyp...]
where the time goes in v2:
time: 102 us; the launch traced here: 101 us
  Pallas kernels  97.9 us (96%)
  local copies, waits for them, and re-layouts  3.46 us (3%)
    pallas_call x1, Pallas kernels, per_device(): pl.pallas_call(functools.partial(kernel, nz, nr), out_shape=jax.ShapeDtyp...  97.9 us
    unnamed x7, local copies, waits for them, and re-layouts  3.46 us

profile of v2, /device:TPU:1, one launch (start us, length us, event | category | flops | bytes accessed | tf_op | source)
XLA Modules:
  0.0 101.3 jit_solution(401114571093722430)
XLA Ops:
  0.0 0.0 copy-start
  0.0 1.0 %copy-done = f32[8,8,8,256]{3,2,1,0:T(8,128)S(1)} copy-done((f32[8,8,8,256]{3,2,1,0:T(8,128)S(1)}, f32[8,8,8,256]{3,2,1,0:T(8,128)}, u32[]{:S(2)}) %copy-start) | copy-done | bytes 524312
  1.0 0.0 copy-start.1
  1.0 0.9 copy-done.1
  2.0 0.0 copy-start.2
  2.0 0.7 copy-done.2
  2.7 97.9 %shard_map.37 = f32[512,256]{1,0:T(8,128)S(1)} custom-call(f32[512,256]{1,0:T(8,128)S(1)} %bitcast.3, f32[3,256]{1,0:T(4,128)S(1)} %copy-done.2, f32[416,128]{1,0:T(8,128)S(1)} %copy-done.1), custom_call_target="tpu_custom_call" | custom-call | tf_op jit(solution)/shard_map/pallas_call | solution.py:773
  100.5 0.8 copy.5
Async XLA Ops:
  0.0 1.0 %copy-start = (f32[8,8,8,256]{3,2,1,0:T(8,128)S(1)}, f32[8,8,8,256]{3,2,1,0:T(8,128)}, u32[]{:S(2)}) copy-start(f32[8,8,8,256]{3,2,1,0:T(8,128)} %param.3) | copy-start | bytes 1572868
  1.0 0.9 copy-start.1
  2.0 0.7 copy-start.2

commit v3 on v2

--- a/solution.py
+++ b/solution.py
@@ -88,27 +88,19 @@
         put(("d", n), column_blocks(np.diag(k)[:, None]))
     for key, table in list(UP.items()) + list(DOWN.items()):
         put(("j",) + key, column_blocks(table))
-    flat = np.concatenate(blocks).reshape(-1, 1).astype(np.float32)
-    wide = np.broadcast_to(flat, (flat.shape[0], LANES))
-    where["pick"] = wide.shape[0] // 8
-    pick = np.zeros((24, LANES), np.float32)
-    for e, (i, j) in enumerate(PAIRS):
-        pick[e, 8 * i + j] = 1.0
-        if j < ITERS:
-            pick[e, 8 * j + i] = 1.0
-    return np.concatenate([wide, pick]), where
+    return np.concatenate(blocks).astype(np.float32), where
 
 
 CONST, WHERE = constant_table()
 
 
-def line(table, values):
+def line(table, values, pairs=None):
     rows, cols = table.shape
     half = cols // 2
     even = [values[k] + values[cols - 1 - k] for k in range(half)]
     odd = [values[k] - values[cols - 1 - k] for k in range(half)]
     out = [None] * rows
-    for i in range(rows // 2):
+    for i in range(rows // 2) if pairs is None else pairs:
         e = o = None
         for k in range(half):
             te = float(np.float32(0.5 * (table[i, k] + table[i, cols - 1 - k])))
@@ -181,10 +173,10 @@
 
 
 def kernel(
-    nz, nr, rhs, stretch, tab, out,
+    nz, nr, rhs, stretch_in, out, stretch, tab,
     x7, d7, r7, inv7, o7, t1, t2, x3, d3, r3, inv3, o3, t3, x1, r1, coef,
     send, recv, send_diag, recv_diag, send_block, recv_block, row_box, gz_box,
-    send_sem, recv_sem, block_send, block_recv, row_send, row_recv, gz_send, gz_recv,
+    load_sem, send_sem, recv_sem, block_send, block_recv, row_send, row_recv, gz_send, gz_recv,
 ):
     gz = lax.axis_index("gz")
     row = lax.axis_index("row")
@@ -215,6 +207,21 @@
     for dz, da in DIRS[4:]:
         pl.semaphore_signal(barrier, inc=1, device_id=at_device(dz, da), device_id_type=mesh_ids)
 
+    loads = [pltpu.make_async_copy(stretch_in, stretch, load_sem.at[2])]
+    for g in range(2):
+        loads.append(
+            pltpu.make_async_copy(rhs.at[:, pl.ds(g * LANES, LANES)], r7.at[pl.ds(g * 512, 512)], load_sem.at[g])
+        )
+    for load in loads:
+        load.start()
+
+    for b, values in enumerate(CONST):
+        block = jnp.full(shape, float(values[0]), jnp.float32)
+        for i in range(1, 8):
+            block = jnp.where(sub == i, float(values[i]), block)
+        tab[rows8(b * 8), :] = block
+    loads[0].wait()
+
     def const(name, j=0):
         return tab[rows8((WHERE[name] + j) * 8), :]
 
@@ -231,12 +238,19 @@
     def coeff(g, k):
         return coef[rows8((g * 3 + k) * 8), :]
 
-    def add_r(field, n, base):
-        lo_at = pl.ds(base, 8, stride=8)
-        hi_at = pl.ds(base + n - 1, 8, stride=8)
+    def add_r(field, n, base, stride=8, inner=False):
+        lo_at = pl.ds(base, 8, stride=stride)
+        hi_at = pl.ds(base + n - 1, 8, stride=stride)
         lo, hi = field[lo_at, :], field[hi_at, :]
-        field[lo_at, :] = lo + jnp.where(in_r > 0, roll(hi, 1), 0.0)
-        field[hi_at, :] = hi + jnp.where(in_r < ER - 1, roll(lo, -1), 0.0)
+        keep = (sub > 0) & (sub < 7) if inner else sub >= 0
+        field[lo_at, :] = lo + jnp.where(keep & (in_r > 0), roll(hi, 1), 0.0)
+        field[hi_at, :] = hi + jnp.where(keep & (in_r < ER - 1), roll(lo, -1), 0.0)
+
+    def with_r(value):
+        from_below = roll(pltpu.roll(value, 1, 0), 1)
+        from_above = roll(pltpu.roll(value, 7, 0), -1)
+        value = value + jnp.where((sub == 0) & (in_r > 0), from_below, 0.0)
+        return value + jnp.where((sub == 7) & (in_r < ER - 1), from_above, 0.0)
 
     def add_a(field, n, base):
         lo_at, hi_at = rows8(base), rows8(base + (n - 1) * 8)
@@ -247,8 +261,8 @@
     def block_at(n, g, iz, ia):
         return rows8(((g * n + iz) * n + ia) * 8)
 
-    def add_z(field, n):
-        for ia in range(n):
+    def add_z(field, n, which=None):
+        for ia in range(n) if which is None else which:
             at = [block_at(n, g, iz, ia) for g, iz in ((0, 0), (1, 0), (0, n - 1), (1, n - 1))]
             lo0, lo1, hi0, hi1 = [field[a, :] for a in at]
             up0, up1, dn0, dn1 = [roll(v, 64) for v in (hi0, hi1, lo0, lo1)]
@@ -270,45 +284,42 @@
             return 0.5 * along if iz in (0, n - 1) else along
         return jnp.where((iz == 0) | (iz == n - 1), 0.5, 1.0) * along
 
+    def along_z(field, image, n, g, ia):
+        base = g * (n * n * 8) + ia * 8
+        got = line(WK[n][1], [field[rows8(base + iz * n * 8), :] for iz in range(n)])
+        c0 = coef[rows8(g * 24), :]
+        for iz in range(n):
+            image[rows8(base + iz * n * 8), :] = c0 * got[iz]
+
+    def rest_values(field, image, n, g, iz, pairs):
+        w, k = WK[n]
+        base = (g * n + iz) * (n * 8)
+        got = line(k, [field[rows8(base + ia * 8), :] for ia in range(n)], pairs)
+        c1 = coef[rows8(g * 24 + 8), :]
+        c2 = coef[rows8(g * 24 + 16), :]
+        scale = tab[rows8((WHERE["w", n] + iz) * 8), :]
+        values = []
+        for ia in sorted(list(pairs) + [n - 1 - p for p in pairs]):
+            at = base + ia * 8
+            part = None
+            for j in range(n):
+                term = const(("k", n), j) * field[pl.ds(at + j, 1), :]
+                part = term if part is None else part + term
+            values.append((ia, (float(w[ia]) * scale) * (image[rows8(at), :] + c1 * got[ia] + c2 * part)))
+        return values
+
     def element(field, image, n, sums, left=None):
-        w, k = WK[n]
-
-        def along_z(i):
-            g, ia = split(i, n)
-            base = g * (n * n * 8) + ia * 8
-            got = line(k, [field[rows8(base + iz * n * 8), :] for iz in range(n)])
-            c0 = coef[rows8(g * 24), :]
-            for iz in range(n):
-                image[rows8(base + iz * n * 8), :] = c0 * got[iz]
+        loop(2 * n, lambda i: along_z(field, image, n, *split(i, n)), n < 8)
 
         def along_rest(i):
             g, iz = split(i, n)
-            base = i * (n * 8)
-            got = line(k, [field[rows8(base + ia * 8), :] for ia in range(n)])
-            c1 = coef[rows8(g * 24 + 8), :]
-            c2 = coef[rows8(g * 24 + 16), :]
-            scale = tab[rows8((WHERE["w", n] + iz) * 8), :]
-            for ia in range(n):
-                at = base + ia * 8
-                part = None
-                for j in range(n):
-                    term = const(("k", n), j) * field[pl.ds(at + j, 1), :]
-                    part = term if part is None else part + term
-                value = (float(w[ia]) * scale) * (image[rows8(at), :] + c1 * got[ia] + c2 * part)
-                if left is not None:
-                    value = shared(iz, ia, n) * left[rows8(at), :] - value
-                image[rows8(at), :] = value
-            if sums and n == 8:
-                add_r(image, n, base)
-                add_a(image, n, base)
-
-        loop(2 * n, along_z, n < 8)
+            for ia, value in rest_values(field, image, n, g, iz, range(n // 2)):
+                at = rows8(i * (n * 8) + ia * 8)
+                image[at, :] = value if left is None else shared(iz, ia, n) * left[at, :] - value
+
         loop(2 * n, along_rest, n < 8)
         if sums:
-            if n == 8:
-                add_z(image, n)
-            else:
-                device_sum(image, n)
+            device_sum(image, n)
 
     def diagonal(field, n):
         w, k = WK[n]
@@ -328,7 +339,7 @@
 
     quarter = in_a
 
-    def pack(field, n, at, at_diag):
+    def pack_a(field, n, at):
         half = n // 2
         for m in range(half):
             rows = rows8(at + m * 8)
@@ -341,15 +352,24 @@
                 to_down = down if k == 0 else jnp.where(quarter == k, down, to_down)
             send[0, rows, :] = to_up
             send[1, rows, :] = to_down
+
+    def pack_z(field, n, at):
+        half = n // 2
+        for m in range(half):
+            rows = rows8(at + m * 8)
             hi = [field[block_at(n, 1, n - 1, ia), :] for ia in (m, m + half)]
             lo = [field[block_at(n, 0, 0, ia), :] for ia in (m, m + half)]
             send[2, rows, :] = jnp.where(low_half, roll(hi[0], 64), hi[1])
             send[3, rows, :] = jnp.where(low_half, lo[0], roll(lo[1], 64))
-        rows = rows8(at_diag)
-        send_diag[0, rows, :] = field[block_at(n, 1, n - 1, n - 1), :]
-        send_diag[1, rows, :] = field[block_at(n, 1, n - 1, 0), :]
-        send_diag[2, rows, :] = field[block_at(n, 0, 0, n - 1), :]
-        send_diag[3, rows, :] = field[block_at(n, 0, 0, 0), :]
+
+    def pack(field, n, at, at_diag):
+        pack_a(field, n, at)
+        pack_z(field, n, at)
+        for d, (g, iz, ia) in enumerate(corners(n)):
+            send_diag[d, rows8(at_diag), :] = field[block_at(n, g, iz, ia), :]
+
+    def corners(n):
+        return ((1, n - 1, n - 1), (1, n - 1, 0), (0, 0, n - 1), (0, 0, 0))
 
     def unpack(field, n, at, at_diag):
         half = n // 2
@@ -382,40 +402,49 @@
         diag_offsets.append(diag_offsets[-1] + len(counts) * 8)
     state = {"next": 0}
 
-    def exchange_start(*fields):
-        turn = state["next"]
-        state["next"] += 1
-        counts = ROUNDS[turn]
-        at, at_diag = offsets[turn], diag_offsets[turn]
-        for field, n in zip(fields, counts):
-            pack(field, n, at, at_diag)
-            at += n * 4
-            at_diag += 8
-        copies = []
-        for d, (dz, da) in enumerate(DIRS):
-            if d < 4:
-                rows = pl.ds(offsets[turn], sum(counts) * 4)
-                src, dst = send.at[d, rows], recv.at[d, rows]
-            else:
-                rows = pl.ds(diag_offsets[turn], len(counts) * 8)
-                src, dst = send_diag.at[d - 4, rows], recv_diag.at[d - 4, rows]
-            copy = pltpu.make_async_remote_copy(
-                src_ref=src, dst_ref=dst, send_sem=send_sem.at[turn, d], recv_sem=recv_sem.at[turn, d],
-                device_id=at_device(dz, da), device_id_type=mesh_ids,
-            )
-            copy.start()
-            copies.append(copy)
-
-        def finish():
-            for copy in copies:
-                copy.wait()
-            at, at_diag = offsets[turn], diag_offsets[turn]
-            for field, n in zip(fields, counts):
-                unpack(field, n, at, at_diag)
+    class Round:
+        def __init__(self, *fields):
+            self.turn = state["next"]
+            state["next"] += 1
+            self.counts = ROUNDS[self.turn]
+            self.at, self.at_diag = offsets[self.turn], diag_offsets[self.turn]
+            self.fields = fields
+            self.copies = []
+
+        def places(self):
+            at, at_diag = self.at, self.at_diag
+            for field, n in zip(self.fields, self.counts):
+                yield field, n, at, at_diag
                 at += n * 4
                 at_diag += 8
 
-        return finish
+        def pack(self):
+            for place in self.places():
+                pack(*place)
+
+        def start(self, which):
+            for d in which:
+                dz, da = DIRS[d]
+                if d < 4:
+                    rows = pl.ds(self.at, sum(self.counts) * 4)
+                    src, dst = send.at[d, rows], recv.at[d, rows]
+                else:
+                    rows = pl.ds(self.at_diag, len(self.counts) * 8)
+                    src, dst = send_diag.at[d - 4, rows], recv_diag.at[d - 4, rows]
+                copy = pltpu.make_async_remote_copy(
+                    src_ref=src, dst_ref=dst, send_sem=send_sem.at[self.turn, d], recv_sem=recv_sem.at[self.turn, d],
+                    device_id=at_device(dz, da), device_id_type=mesh_ids,
+                )
+                copy.start()
+                self.copies.append(copy)
+
+        def finish(self):
+            for copy in self.copies:
+                copy.wait()
+            for place in self.places():
+                unpack(*place)
+
+    LATE_FIRST = (4, 5, 6, 7, 0, 1, 2, 3)
 
     def block_start(turn, at, count):
         copies = []
@@ -446,11 +475,62 @@
         return jnp.concatenate([top, bottom], axis=0)
 
     def exchange(*fields):
-        exchange_start(*fields)()
+        turn = Round(*fields)
+        turn.pack()
+        turn.start(LATE_FIRST)
+        turn.finish()
 
     def apply(field, image, n):
-        element(field, image, n, True)
-        exchange(image)
+        if n == 8:
+            apply_fine(field, image)
+        else:
+            element(field, image, n, True)
+            exchange(image)
+
+    def apply_fine(field, image):
+        turn = Round(image)
+        for g in range(2):
+            for ia in (0, 7):
+                along_z(field, image, 8, g, ia)
+        for d, (g, iz) in enumerate(((1, 7), (0, 0))):
+            (_, first), (_, last) = rest_values(field, image, 8, g, iz, (0,))
+            send_diag[2 * d, rows8(turn.at_diag), :] = with_r(last)
+            send_diag[2 * d + 1, rows8(turn.at_diag), :] = with_r(first)
+        turn.start((4, 5, 6, 7))
+
+        @pl.loop(0, 16)
+        def _(i):
+            g, iz = split(i, 8)
+            for ia, value in rest_values(field, image, 8, g, iz, (0,)):
+                image[rows8(i * 64 + ia * 8), :] = value
+
+        for g in range(2):
+            for ia in (0, 7):
+                add_r(image, 8, g * 512 + ia * 8, 64)
+        for i in range(16):
+            add_a(image, 8, i * 64)
+        add_z(image, 8, (0, 7))
+        pack_a(image, 8, turn.at)
+        turn.start((0, 1))
+
+        @pl.loop(0, 12)
+        def _(i):
+            g, ia = split(i, 6)
+            along_z(field, image, 8, g, ia + 1)
+
+        def inner(i):
+            g, iz = split(i, 8)
+            for ia, value in rest_values(field, image, 8, g, iz, (1, 2, 3)):
+                image[rows8(i * 64 + ia * 8), :] = value
+            add_r(image, 8, i * 64, 8, True)
+
+        inner(0)
+        inner(15)
+        pack_z(image, 8, turn.at)
+        turn.start((2, 3))
+        pl.loop(1, 15)(inner)
+        add_z(image, 8, range(1, 7))
+        turn.finish()
 
     def blocks(n, body):
         def step(i):
@@ -465,12 +545,8 @@
         keep = jnp.concatenate([as_float(live(n))] * 8, axis=0)
         return keep * value
 
-    @pl.loop(0, 8)
-    def _(i):
-        rows = pl.ds(pl.multiple_of(i * 64, 64), 64)
-        for g in range(2):
-            r7[pl.ds(pl.multiple_of(g * 512 + i * 64, 64), 64), :] = rhs[rows, pl.ds(g * LANES, LANES)]
-
+    for load in loads[1:]:
+        load.wait()
     device_sum(r7, 8)
     diagonal(inv7, 8)
     device_sum(inv7, 8)
@@ -479,10 +555,12 @@
     for k in range(3):
         rows = jnp.where(sub < 2, coeff(0, k), coeff(1, k))
         send_block[rows8(k * 8), :] = jnp.where(sub % 2 == 0, rows, roll(rows, 64))
+    first_round = Round(r7, inv7, inv3)
+    first_round.pack()
     pl.semaphore_wait(barrier, (nr - 1) + (nz - 1) + 4)
-    finish_first = exchange_start(r7, inv7, inv3)
+    first_round.start(LATE_FIRST)
     stretch_copies = block_start(0, 0, 24)
-    finish_first()
+    first_round.finish()
 
     def invert(inv, n):
         keep = jnp.concatenate([live(n)] * 8, axis=0)
@@ -652,7 +730,13 @@
         total = (tiles[2 * t], tiles[2 * t + 1])
         for amount in (64, 32, 16, 8, 4, 2, 1):
             total = add2(total, tuple(roll(part, amount) for part in total))
-        pick = tab[rows8((WHERE["pick"] + t) * 8), :] > 0.0
+        pick = sub < 0
+        for e in range(8 * t, min(8 * t + 8, len(PAIRS))):
+            i, j = PAIRS[e]
+            spot = lane == 8 * i + j
+            if j < ITERS:
+                spot = spot | (lane == 8 * j + i)
+            pick = pick | ((sub == e % 8) & spot)
         for half in range(2):
             sent[half] = sent[half] + jnp.sum(jnp.where(pick, total[half], 0.0), axis=0, keepdims=True)
     for half in range(2):
@@ -773,9 +857,10 @@
     out = pl.pallas_call(
         functools.partial(kernel, nz, nr),
         out_shape=jax.ShapeDtypeStruct((nodes, elems), jnp.float32),
-        in_specs=[pl.BlockSpec(memory_space=pltpu.VMEM)] * 3,
+        in_specs=[pl.BlockSpec(memory_space=pltpu.HBM)] * 2,
         out_specs=pl.BlockSpec(memory_space=pltpu.VMEM),
-        scratch_shapes=[field(1024)] * 5
+        scratch_shapes=[pltpu.VMEM((3, elems), jnp.float32), field(CONST.shape[0] * 8)]
+        + [field(1024)] * 5
         + [field(512), field(256)]
         + [field(256)] * 5
         + [field(128)]
@@ -790,6 +875,7 @@
             pltpu.VMEM((8, 32, LANES), jnp.float32),
             pltpu.VMEM((nr, 2, LANES), jnp.float32),
             pltpu.VMEM((nz, 2, LANES), jnp.float32),
+            pltpu.SemaphoreType.DMA((3,)),
             pltpu.SemaphoreType.DMA((len(ROUNDS), 8)),
             pltpu.SemaphoreType.DMA((len(ROUNDS), 8)),
             pltpu.SemaphoreType.DMA((2, 8)),
@@ -802,7 +888,7 @@
         compiler_params=pltpu.CompilerParams(
             collective_id=0, has_side_effects=True, vmem_limit_bytes=32 * 1024 * 1024
         ),
-    )(rhs_local.reshape(nodes, elems), stretch, jnp.asarray(CONST))
+    )(rhs_local.reshape(nodes, elems), stretch)
     return out.reshape(rhs_local.shape)
 
 

time: 102 us -> 89.9 us (0.88)
  Pallas kernels: 97.9 us -> 87.1 us
    pallas_call x1, Pallas kernels: 97.9 us -> 87.1 us  [per_device(): pl.pallas_call(functools.partial(kernel, nz, nr), out_shape=jax.ShapeDtyp...]
    unnamed x7 -> x5, local copies, waits for them, and re-layouts: 3.46 us -> 2.52 us
where the time goes in v3:
time: 89.9 us; the launch traced here: 89.7 us
  Pallas kernels  87.1 us (97%)
  local copies, waits for them, and re-layouts  2.52 us (3%)
    pallas_call x1, Pallas kernels, per_device(): pl.pallas_call(functools.partial(kernel, nz, nr), out_shape=jax.ShapeDtyp...  87.1 us
    unnamed x5, local copies, waits for them, and re-layouts  2.52 us

profile of v3, /device:TPU:1, one launch (start us, length us, event | category | flops | bytes accessed | tf_op | source)
XLA Modules:
  0.0 89.7 jit_solution(14461192513357363117)
XLA Ops:
  0.0 0.0 copy-start
  0.0 1.0 %copy-done = f32[8,8,8,256]{3,2,1,0:T(8,128)S(1)} copy-done((f32[8,8,8,256]{3,2,1,0:T(8,128)S(1)}, f32[8,8,8,256]{3,2,1,0:T(8,128)}, u32[]{:S(2)}) %copy-start) | copy-done | bytes 524312
  1.0 0.0 copy-start.1
  1.0 0.7 copy-done.1
  1.7 87.1 %shard_map.28 = f32[512,256]{1,0:T(8,128)S(1)} custom-call(f32[512,256]{1,0:T(8,128)S(1)} %bitcast.3, f32[3,256]{1,0:T(4,128)S(1)} %copy-done.1), custom_call_target="tpu_custom_call" | custom-call | tf_op jit(solution)/shard_map/pallas_call | solution.py:857
  88.9 0.8 copy.4
Async XLA Ops:
  0.0 1.0 %copy-start = (f32[8,8,8,256]{3,2,1,0:T(8,128)S(1)}, f32[8,8,8,256]{3,2,1,0:T(8,128)}, u32[]{:S(2)}) copy-start(f32[8,8,8,256]{3,2,1,0:T(8,128)} %param.2) | copy-start | bytes 1572868
  1.0 0.7 copy-start.1

commit v4 on v3

--- a/solution.py
+++ b/solution.py
@@ -25,7 +25,8 @@
 RHO2 = 1.0 / (2.0 * THETA / DELTA - RHO)
 
 DIRS = ((0, 1), (0, -1), (1, 0), (-1, 0), (1, 1), (1, -1), (-1, 1), (-1, -1))
-ROUNDS = ((8, 8, 4), (8,), (4,), (4,), (2,), (4,), (4,), (8,), (8,))
+FAR_DIRS = tuple((z, a) for z in (2, -2, 1, -1, 0) for a in (2, -2, 1, -1, 0) if (z, a) != (0, 0))
+ROUNDS = ((8, 8, 4), (8,), (4,), (4,), (4,) * 6, (4,), (8,), (8,))
 SCALE = 16.0
 TINY = 1e-13
 
@@ -175,8 +176,8 @@
 def kernel(
     nz, nr, rhs, stretch_in, out, stretch, tab,
     x7, d7, r7, inv7, o7, t1, t2, x3, d3, r3, inv3, o3, t3, x1, r1, coef,
-    send, recv, send_diag, recv_diag, send_block, recv_block, row_box, gz_box,
-    load_sem, send_sem, recv_sem, block_send, block_recv, row_send, row_recv, gz_send, gz_recv,
+    vertex, lifted, images, send, recv, send_diag, recv_diag, send_block, recv_block, send_point, recv_point, row_box, gz_box,
+    load_sem, send_sem, recv_sem, block_send, block_recv, point_send, point_recv, row_send, row_recv, gz_send, gz_recv,
 ):
     gz = lax.axis_index("gz")
     row = lax.axis_index("row")
@@ -204,7 +205,8 @@
     def _(o):
         pl.semaphore_signal(barrier, inc=1, device_id=(lax.rem(gz + o, nz), row), device_id_type=mesh_ids)
 
-    for dz, da in DIRS[4:]:
+    askew = [d for d in FAR_DIRS if d[0] != 0 and d[1] != 0]
+    for dz, da in askew:
         pl.semaphore_signal(barrier, inc=1, device_id=at_device(dz, da), device_id_type=mesh_ids)
 
     loads = [pltpu.make_async_copy(stretch_in, stretch, load_sem.at[2])]
@@ -446,12 +448,11 @@
 
     LATE_FIRST = (4, 5, 6, 7, 0, 1, 2, 3)
 
-    def block_start(turn, at, count):
+    def send_all(dirs, src, dst, sends, recvs):
         copies = []
-        for d, (dz, da) in enumerate(DIRS):
+        for d, (dz, da) in enumerate(dirs):
             copy = pltpu.make_async_remote_copy(
-                src_ref=send_block.at[pl.ds(at, count)], dst_ref=recv_block.at[d, pl.ds(at, count)],
-                send_sem=block_send.at[turn, d], recv_sem=block_recv.at[turn, d],
+                src_ref=src, dst_ref=dst.at[d], send_sem=sends.at[d], recv_sem=recvs.at[d],
                 device_id=at_device(dz, da), device_id_type=mesh_ids,
             )
             copy.start()
@@ -557,9 +558,9 @@
         send_block[rows8(k * 8), :] = jnp.where(sub % 2 == 0, rows, roll(rows, 64))
     first_round = Round(r7, inv7, inv3)
     first_round.pack()
-    pl.semaphore_wait(barrier, (nr - 1) + (nz - 1) + 4)
+    pl.semaphore_wait(barrier, (nr - 1) + (nz - 1) + len(askew))
     first_round.start(LATE_FIRST)
-    stretch_copies = block_start(0, 0, 24)
+    stretch_copies = send_all(DIRS, send_block, recv_block, block_send, block_recv)
     first_round.finish()
 
     def invert(inv, n):
@@ -618,7 +619,7 @@
         loop(2 * nf, along_z, nf < 8)
         loop(2 * nc, along_a, nf < 8)
 
-    def prolong(coarse, nc, nf, fields, tz, ta):
+    def prolong(coarse, nc, nf, fields, tz, ta, add=True):
         table = UP[nc, nf]
 
         def along_a(i):
@@ -635,7 +636,7 @@
             for iz in range(nf):
                 at = rows8((g * nf + iz) * (nf * 8) + ia * 8)
                 for field in fields:
-                    field[at, :] = field[at, :] + got[iz]
+                    field[at, :] = field[at, :] + got[iz] if add else got[iz]
 
         loop(2 * nc, along_a, nf < 8)
         loop(2 * nf, along_z, nf < 8)
@@ -654,9 +655,20 @@
     element(d3, o3, 4, False, left=r3)
 
     restrict(o3, 4, 2, r1, t3, t2)
-    device_sum(r1, 2)
-    exchange(r1)
-    r1[...] = masked(2, r1[...])
+    per_z = []
+    for iz in range(2):
+        per_a = []
+        for ia in range(2):
+            at = [((g * 2 + iz) * 2 + ia) * 8 for g in range(2)]
+            per_r = []
+            for ir in range(2):
+                rows = jnp.where(sub < 2, r1[pl.ds(at[0] + ir, 1), :], r1[pl.ds(at[1] + ir, 1), :])
+                rows = jnp.where(sub % 2 == 0, rows, roll(rows, 64))
+                per_r.append(jnp.where((sub < 4) & low_half, rows, 0.0))
+            per_a.append(per_r[0] + roll(per_r[1], 1))
+        per_z.append(per_a[0] + roll(per_a[1], ER))
+    send_point[...] = per_z[0] + pltpu.roll(per_z[1], 1, 0)
+    point_copies = send_all(FAR_DIRS, send_point, recv_point, point_send, point_recv)
 
     for copy in stretch_copies:
         copy.wait()
@@ -687,24 +699,36 @@
             total = flux if total is None else total + flux
         return jnp.where(inside, (1.0 / SCALE) * total, 0.0)
 
-    def vertex_row(g, iz, odd):
-        inner = jnp.broadcast_to(r1[pl.ds(((g * 2 + iz) * 2) * 8, 1), :], shape)
-        outer = jnp.broadcast_to(r1[pl.ds(((g * 2 + iz) * 2 + 1) * 8, 1), :], shape)
-        shift = 64 if odd else 0
-        return jnp.where(low_half, roll(inner, shift), roll(outer, shift + ER))
-
-    block = vertex_row(1, 1, True)
-    for z in range(EZ):
-        block = jnp.where(sub == z, vertex_row(z // 2, 0, z % 2 == 1), block)
-    send_block[rows8(24), :] = block
-    for copy in block_start(1, 24, 8):
+    def summed_points():
+        def from_device(dz, da):
+            if (dz, da) == (0, 0):
+                return send_point[...]
+            return recv_point[FAR_DIRS.index((-dz, -da))]
+
+        left, right = [], []
+        for dz in (-2, -1, 0, 1, 2):
+            far_left, near_left, mine, near_right, far_right = [from_device(dz, da) for da in (-2, -1, 0, 1, 2)]
+            turned = roll(mine, 64)
+            left.append(near_left + jnp.where(low_half, jnp.where(lane < ER, roll(far_left, 64), 0.0), turned))
+            far_right = jnp.where((lane >= 64) & (lane < 64 + ER), roll(far_right, 64), 0.0)
+            right.append(near_right + jnp.where(lane < ER, turned, far_right))
+        halves_of = []
+        for far_low, near_low, mine, near_high, far_high in (left, right):
+            turned, far_low, far_high = [pltpu.roll(v, 4, 0) for v in (mine, far_low, far_high)]
+            top = near_low + jnp.where(sub >= 4, turned, jnp.where(sub == 0, far_low, 0.0))
+            bottom = near_high + jnp.where(sub == 0, turned, jnp.where(sub == 4, far_high, 0.0))
+            halves_of.append(jnp.concatenate([top, bottom], axis=0))
+        return jnp.where(inside, jnp.concatenate(halves_of, axis=1), 0.0)
+
+    for copy in point_copies:
         copy.wait()
-
-    basis = [wide(24)]
+    basis = [summed_points()]
     slopes = [differences(basis[0])]
     for k in range(1, ITERS):
         basis.append(vertex_image(slopes[-1]))
         slopes.append(differences(basis[-1]))
+    for k in range(ITERS):
+        vertex[k] = basis[k]
 
     own = (sub >= 4) & jnp.logical_not(low_half)
     roots = [jnp.where(own, jnp.sqrt(edge[0:8, 0:LANES]), 0.0) for edge in edges]
@@ -760,6 +784,38 @@
             parts = [add2(parts[k], parts[k + half]) for k in range(half)] + parts[2 * half :]
         return parts[0]
 
+    @pl.loop(0, ITERS)
+    def _(k):
+        value = vertex[k]
+        for ia in range(2):
+            at_node = []
+            for ir in range(2):
+                back = 64 + ER * ia + ir
+                at_node.append([pltpu.roll(value, (shift - back) % 256, 1)[:, 0:LANES] for shift in (0, 64)])
+            for g in range(2):
+                for iz in range(2):
+                    row_at = 4 + 2 * g + iz
+                    pair = [
+                        jnp.where(
+                            low_half,
+                            jnp.broadcast_to(v[0][row_at : row_at + 1], shape),
+                            jnp.broadcast_to(v[1][row_at + 1 : row_at + 2], shape),
+                        )
+                        for v in at_node
+                    ]
+                    x1[block_at(2, g, iz, ia), :] = jnp.where(sub == 0, pair[0], jnp.where(sub == 1, pair[1], 0.0))
+        prolong(x1, 2, 4, (lifted.at[k],), t3, t2, False)
+
+    lifted[ITERS] = d3[...]
+
+    @pl.loop(0, ITERS + 1)
+    def _(k):
+        element(lifted.at[k], images.at[k], 4, True)
+
+    lifted_round = Round(*[images.at[k] for k in range(ITERS + 1)])
+    lifted_round.pack()
+    lifted_round.start(LATE_FIRST)
+
     wait_for(row_box, nr, row_recv)
     total = total_of(row_box, nr)
     for half in range(2):
@@ -772,6 +828,7 @@
             device_id=(lax.rem(gz + o, nz), row), device_id_type=mesh_ids,
         ).start()
 
+    lifted_round.finish()
     wait_for(gz_box, nz, gz_recv)
     total = total_of(gz_box, nz)
     wait_for(row_box, nr, row_send)
@@ -797,29 +854,20 @@
         rest = add2(system, (-taken[0], -taken[1]))
         system = [jnp.where(sub == p, scaled[half], rest[half]) for half in range(2)]
 
-    solved = None
+    factors = []
     for k in range(ITERS):
-        factor = jnp.broadcast_to(jnp.broadcast_to(system[0][k : k + 1, :], (16, LANES))[:, ITERS : ITERS + 1], (16, 256))
-        term = factor * basis[k]
-        solved = term if solved is None else solved + term
-
-    for ia in range(2):
-        at_node = []
-        for ir in range(2):
-            back = 64 + ER * ia + ir
-            at_node.append([pltpu.roll(solved, (shift - back) % 256, 1)[:, 0:LANES] for shift in (0, 64)])
-        for g in range(2):
-            for iz in range(2):
-                row_at = 4 + 2 * g + iz
-                pair = [
-                    jnp.where(low_half, jnp.broadcast_to(v[0][row_at : row_at + 1], shape), jnp.broadcast_to(v[1][row_at + 1 : row_at + 2], shape))
-                    for v in at_node
-                ]
-                x1[block_at(2, g, iz, ia), :] = jnp.where(sub == 0, pair[0], jnp.where(sub == 1, pair[1], 0.0))
-
-    prolong(x1, 2, 4, (d3, x3), t3, t2)
-    apply(d3, o3, 4)
-    r3[...] = r3[...] - o3[...]
+        factor = jnp.broadcast_to(system[0][k : k + 1, :], shape)[:, ITERS : ITERS + 1]
+        factors.append(jnp.concatenate([jnp.broadcast_to(factor, shape)] * 8, axis=0))
+
+    def correct(at):
+        gain, image = x3[at, :], images[ITERS, at, :]
+        for k in range(ITERS):
+            gain = gain + factors[k] * lifted[k, at, :]
+            image = image + factors[k] * images[k, at, :]
+        x3[at, :] = gain
+        r3[at, :] = r3[at, :] - image
+
+    blocks(4, correct)
     smooth_first(inv3, r3, d3, 4)
     apply(d3, o3, 4)
     smooth_second(inv3, r3, d3, x3, o3, 4, True, False)
@@ -867,19 +915,26 @@
         + [field(64)] * 2
         + [field(48)]
         + [
+            pltpu.VMEM((ITERS, 16, 256), jnp.float32),
+            pltpu.VMEM((ITERS + 1, 256, LANES), jnp.float32),
+            pltpu.VMEM((ITERS + 1, 256, LANES), jnp.float32),
             pltpu.VMEM((4, face_rows, LANES), jnp.float32),
             pltpu.VMEM((4, face_rows, LANES), jnp.float32),
             pltpu.VMEM((4, diag_rows, LANES), jnp.float32),
             pltpu.VMEM((4, diag_rows, LANES), jnp.float32),
-            pltpu.VMEM((32, LANES), jnp.float32),
-            pltpu.VMEM((8, 32, LANES), jnp.float32),
+            pltpu.VMEM((24, LANES), jnp.float32),
+            pltpu.VMEM((8, 24, LANES), jnp.float32),
+            pltpu.VMEM((8, LANES), jnp.float32),
+            pltpu.VMEM((len(FAR_DIRS), 8, LANES), jnp.float32),
             pltpu.VMEM((nr, 2, LANES), jnp.float32),
             pltpu.VMEM((nz, 2, LANES), jnp.float32),
             pltpu.SemaphoreType.DMA((3,)),
             pltpu.SemaphoreType.DMA((len(ROUNDS), 8)),
             pltpu.SemaphoreType.DMA((len(ROUNDS), 8)),
-            pltpu.SemaphoreType.DMA((2, 8)),
-            pltpu.SemaphoreType.DMA((2, 8)),
+            pltpu.SemaphoreType.DMA((8,)),
+            pltpu.SemaphoreType.DMA((8,)),
+            pltpu.SemaphoreType.DMA((len(FAR_DIRS),)),
+            pltpu.SemaphoreType.DMA((len(FAR_DIRS),)),
             pltpu.SemaphoreType.DMA,
             pltpu.SemaphoreType.DMA,
             pltpu.SemaphoreType.DMA,

time: 89.9 us -> 80.6 us (0.90)
  Pallas kernels: 87.1 us -> 77.9 us
    pallas_call x1, Pallas kernels: 87.1 us -> 77.9 us  [per_device(): pl.pallas_call(functools.partial(kernel, nz, nr), out_shape=jax.ShapeDtyp...]
where the time goes in v4:
time: 80.6 us; the launch traced here: 80.4 us
  Pallas kernels  77.9 us (97%)
  local copies, waits for them, and re-layouts  2.52 us (3%)
    pallas_call x1, Pallas kernels, per_device(): pl.pallas_call(functools.partial(kernel, nz, nr), out_shape=jax.ShapeDtyp...  77.9 us
    unnamed x5, local copies, waits for them, and re-layouts  2.52 us

profile of v4, /device:TPU:1, one launch (start us, length us, event | category | flops | bytes accessed | tf_op | source)
XLA Modules:
  0.0 80.4 jit_solution(1034274969350602520)
XLA Ops:
  0.0 0.0 copy-start
  0.0 1.0 %copy-done = f32[8,8,8,256]{3,2,1,0:T(8,128)S(1)} copy-done((f32[8,8,8,256]{3,2,1,0:T(8,128)S(1)}, f32[8,8,8,256]{3,2,1,0:T(8,128)}, u32[]{:S(2)}) %copy-start) | copy-done | bytes 524312
  1.0 0.0 copy-start.1
  1.0 0.7 copy-done.1
  1.7 77.9 %shard_map.28 = f32[512,256]{1,0:T(8,128)S(1)} custom-call(f32[512,256]{1,0:T(8,128)S(1)} %bitcast.3, f32[3,256]{1,0:T(4,128)S(1)} %copy-done.1), custom_call_target="tpu_custom_call" | custom-call | tf_op jit(solution)/shard_map/pallas_call | solution.py:905
  79.6 0.8 copy.4
Async XLA Ops:
  0.0 1.0 %copy-start = (f32[8,8,8,256]{3,2,1,0:T(8,128)S(1)}, f32[8,8,8,256]{3,2,1,0:T(8,128)}, u32[]{:S(2)}) copy-start(f32[8,8,8,256]{3,2,1,0:T(8,128)} %param.2) | copy-start | bytes 1572868
  1.0 0.7 copy-start.1

commit v5 on v4

--- a/solution.py
+++ b/solution.py
@@ -129,7 +129,7 @@
         for i in range(count):
             body(i)
     else:
-        pl.loop(0, count)(body)
+        pl.loop(0, count, unroll=2)(body)
 
 
 def split(i, size):
@@ -244,15 +244,15 @@
         lo_at = pl.ds(base, 8, stride=stride)
         hi_at = pl.ds(base + n - 1, 8, stride=stride)
         lo, hi = field[lo_at, :], field[hi_at, :]
-        keep = (sub > 0) & (sub < 7) if inner else sub >= 0
+        keep = (sub % n > 0) & (sub % n < n - 1) if inner else sub >= 0
         field[lo_at, :] = lo + jnp.where(keep & (in_r > 0), roll(hi, 1), 0.0)
         field[hi_at, :] = hi + jnp.where(keep & (in_r < ER - 1), roll(lo, -1), 0.0)
 
-    def with_r(value):
-        from_below = roll(pltpu.roll(value, 1, 0), 1)
-        from_above = roll(pltpu.roll(value, 7, 0), -1)
+    def with_r(value, n):
+        from_below = roll(pltpu.roll(value, 9 - n, 0), 1)
+        from_above = roll(pltpu.roll(value, n - 1, 0), -1)
         value = value + jnp.where((sub == 0) & (in_r > 0), from_below, 0.0)
-        return value + jnp.where((sub == 7) & (in_r < ER - 1), from_above, 0.0)
+        return value + jnp.where((sub == n - 1) & (in_r < ER - 1), from_above, 0.0)
 
     def add_a(field, n, base):
         lo_at, hi_at = rows8(base), rows8(base + (n - 1) * 8)
@@ -373,30 +373,35 @@
     def corners(n):
         return ((1, n - 1, n - 1), (1, n - 1, 0), (0, 0, n - 1), (0, 0, 0))
 
-    def unpack(field, n, at, at_diag):
+    def unpack(field, n, at, at_diag, fix=None):
         half = n // 2
 
-        def add(where, keep, value):
-            field[where, :] = field[where, :] + jnp.where(keep, value, 0.0)
+        def add(place, keep, value):
+            value = jnp.where(keep, value, 0.0)
+            if fix is not None:
+                fix(place, value)
+            else:
+                where = block_at(n, *place)
+                field[where, :] = field[where, :] + value
 
         for m in range(half):
             rows = rows8(at + m * 8)
             got = [recv[d, rows, :] for d in range(4)]
             for k in range(4):
                 g, iz = divmod(m + k * half, n)
-                add(block_at(n, g, iz, 0), in_a == 0, roll(got[0], -16 * k))
-                add(block_at(n, g, iz, n - 1), in_a == EA - 1, roll(got[1], 48 - 16 * k))
+                add((g, iz, 0), in_a == 0, roll(got[0], -16 * k))
+                add((g, iz, n - 1), in_a == EA - 1, roll(got[1], 48 - 16 * k))
         for m in range(half):
             rows = rows8(at + m * 8)
             got = [recv[d, rows, :] for d in range(4)]
             for k in range(2):
-                add(block_at(n, 0, 0, m + k * half), low_half, roll(got[2], 64 * k))
-                add(block_at(n, 1, n - 1, m + k * half), jnp.logical_not(low_half), roll(got[3], 64 - 64 * k))
+                add((0, 0, m + k * half), low_half, roll(got[2], 64 * k))
+                add((1, n - 1, m + k * half), jnp.logical_not(low_half), roll(got[3], 64 - 64 * k))
         rows = rows8(at_diag)
-        add(block_at(n, 0, 0, 0), lane < 16, roll(recv_diag[0, rows, :], 16))
-        add(block_at(n, 0, 0, n - 1), (lane >= 48) & (lane < 64), roll(recv_diag[1, rows, :], -16))
-        add(block_at(n, 1, n - 1, 0), (lane >= 64) & (lane < 80), roll(recv_diag[2, rows, :], 16))
-        add(block_at(n, 1, n - 1, n - 1), lane >= 112, roll(recv_diag[3, rows, :], -16))
+        add((0, 0, 0), lane < 16, roll(recv_diag[0, rows, :], 16))
+        add((0, 0, n - 1), (lane >= 48) & (lane < 64), roll(recv_diag[1, rows, :], -16))
+        add((1, n - 1, 0), (lane >= 64) & (lane < 80), roll(recv_diag[2, rows, :], 16))
+        add((1, n - 1, n - 1), lane >= 112, roll(recv_diag[3, rows, :], -16))
 
     offsets, diag_offsets = [0], [0]
     for counts in ROUNDS:
@@ -440,11 +445,11 @@
                 copy.start()
                 self.copies.append(copy)
 
-        def finish(self):
+        def finish(self, fix=None):
             for copy in self.copies:
                 copy.wait()
             for place in self.places():
-                unpack(*place)
+                unpack(*place, fix)
 
     LATE_FIRST = (4, 5, 6, 7, 0, 1, 2, 3)
 
@@ -481,57 +486,56 @@
         turn.start(LATE_FIRST)
         turn.finish()
 
-    def apply(field, image, n):
-        if n == 8:
-            apply_fine(field, image)
-        else:
-            element(field, image, n, True)
-            exchange(image)
-
-    def apply_fine(field, image):
+    def apply(field, image, n, during, fix):
         turn = Round(image)
+        ends = (0, n - 1)
         for g in range(2):
-            for ia in (0, 7):
-                along_z(field, image, 8, g, ia)
-        for d, (g, iz) in enumerate(((1, 7), (0, 0))):
-            (_, first), (_, last) = rest_values(field, image, 8, g, iz, (0,))
-            send_diag[2 * d, rows8(turn.at_diag), :] = with_r(last)
-            send_diag[2 * d + 1, rows8(turn.at_diag), :] = with_r(first)
+            for ia in ends:
+                along_z(field, image, n, g, ia)
+        for d, (g, iz) in enumerate(((1, n - 1), (0, 0))):
+            (_, first), (_, last) = rest_values(field, image, n, g, iz, (0,))
+            send_diag[2 * d, rows8(turn.at_diag), :] = with_r(last, n)
+            send_diag[2 * d + 1, rows8(turn.at_diag), :] = with_r(first, n)
         turn.start((4, 5, 6, 7))
 
-        @pl.loop(0, 16)
-        def _(i):
-            g, iz = split(i, 8)
-            for ia, value in rest_values(field, image, 8, g, iz, (0,)):
-                image[rows8(i * 64 + ia * 8), :] = value
-
-        for g in range(2):
-            for ia in (0, 7):
-                add_r(image, 8, g * 512 + ia * 8, 64)
-        for i in range(16):
-            add_a(image, 8, i * 64)
-        add_z(image, 8, (0, 7))
-        pack_a(image, 8, turn.at)
+        def outer(i):
+            g, iz = split(i, n)
+            for ia, value in rest_values(field, image, n, g, iz, (0,)):
+                image[rows8(i * (n * 8) + ia * 8), :] = value
+
+        loop(2 * n, outer, n < 8)
+        for q in range(2 * n // 8):
+            for ia in ends:
+                add_r(image, n, q * (n * 64) + ia * 8, n * 8)
+        for i in range(2 * n):
+            add_a(image, n, i * n * 8)
+        add_z(image, n, ends)
+        pack_a(image, n, turn.at)
         turn.start((0, 1))
 
-        @pl.loop(0, 12)
-        def _(i):
-            g, ia = split(i, 6)
-            along_z(field, image, 8, g, ia + 1)
-
-        def inner(i):
-            g, iz = split(i, 8)
-            for ia, value in rest_values(field, image, 8, g, iz, (1, 2, 3)):
-                image[rows8(i * 64 + ia * 8), :] = value
-            add_r(image, 8, i * 64, 8, True)
-
+        def inner_z(i):
+            g, ia = split(i, n - 2)
+            along_z(field, image, n, g, ia + 1)
+
+        loop(2 * (n - 2), inner_z, n < 8)
+
+        def inner(q):
+            for part in range(8 // n):
+                i = q * (8 // n) + part
+                g, iz = split(i, n)
+                for ia, value in rest_values(field, image, n, g, iz, range(1, n // 2)):
+                    image[rows8(i * (n * 8) + ia * 8), :] = value
+            add_r(image, n, q * 64, 8, True)
+
+        groups = 2 * n * n // 8
         inner(0)
-        inner(15)
-        pack_z(image, 8, turn.at)
+        inner(groups - 1)
+        pack_z(image, n, turn.at)
         turn.start((2, 3))
-        pl.loop(1, 15)(inner)
-        add_z(image, 8, range(1, 7))
-        turn.finish()
+        loop(groups - 2, lambda q: inner(q + 1), n < 8)
+        add_z(image, n, range(1, n - 1))
+        during()
+        turn.finish(fix)
 
     def blocks(n, body):
         def step(i):
@@ -580,17 +584,33 @@
 
         blocks(n, body)
 
-    def smooth_second(inv, r, d, x, image, n, add, keep_r=True):
+    def smooth_second(inv, r, d, x, image, n, result=None):
         def body(at):
             step = d[at, :]
             left = r[at, :] - image[at, :]
             second = (RHO2 * RHO) * step + (2.0 * RHO2 / DELTA) * (inv[at, :] * left)
-            x[at, :] = (x[at, :] + (step + second)) if add else step + second
-            if keep_r:
+            if result is None:
+                x[at, :] = step + second
                 d[at, :] = second
                 r[at, :] = left
-
-        blocks(n, body)
+            else:
+                result(at, x[at, :] + (step + second))
+
+        def fix(place, value):
+            at = block_at(n, *place)
+            change = (2.0 * RHO2 / DELTA) * (inv[at, :] * value)
+            if result is None:
+                r[at, :] = r[at, :] - value
+                d[at, :] = d[at, :] - change
+                x[at, :] = x[at, :] - change
+            elif n == 8:
+                g, iz, ia = place
+                spot = rows8((iz * 8 + ia) * 8), pl.ds(g * LANES, LANES)
+                out[spot] = out[spot] - change
+            else:
+                x[at, :] = x[at, :] - change
+
+        apply(d, image, n, lambda: blocks(n, body), fix)
 
     def r_line(name, field, at, count):
         part = None
@@ -642,16 +662,14 @@
         loop(2 * nf, along_z, nf < 8)
 
     smooth_first(inv7, r7, d7, 8)
-    apply(d7, o7, 8)
-    smooth_second(inv7, r7, d7, x7, o7, 8, False)
+    smooth_second(inv7, r7, d7, x7, o7, 8)
     element(d7, o7, 8, False, left=r7)
 
     restrict(o7, 8, 4, r3, t1, t2)
     device_sum(r3, 4)
     exchange(r3)
     smooth_first(inv3, r3, d3, 4)
-    apply(d3, o3, 4)
-    smooth_second(inv3, r3, d3, x3, o3, 4, False)
+    smooth_second(inv3, r3, d3, x3, o3, 4)
     element(d3, o3, 4, False, left=r3)
 
     restrict(o3, 4, 2, r1, t3, t2)
@@ -869,26 +887,32 @@
 
     blocks(4, correct)
     smooth_first(inv3, r3, d3, 4)
-    apply(d3, o3, 4)
-    smooth_second(inv3, r3, d3, x3, o3, 4, True, False)
+
+    def keep_x3(at, value):
+        x3[at, :] = value
+
+    smooth_second(inv3, r3, d3, x3, o3, 4, keep_x3)
 
     prolong(x3, 4, 8, (d7, x7), t1, t2)
-    apply(d7, o7, 8)
 
     def before_last(at):
         left = r7[at, :] - o7[at, :]
         r7[at, :] = left
         d7[at, :] = (1.0 / THETA) * (inv7[at, :] * left)
 
-    blocks(8, before_last)
-    apply(d7, o7, 8)
-    smooth_second(inv7, r7, d7, x7, o7, 8, True, False)
-
-    @pl.loop(0, 8)
-    def _(i):
-        rows = pl.ds(pl.multiple_of(i * 64, 64), 64)
-        for g in range(2):
-            out[rows, pl.ds(g * LANES, LANES)] = x7[pl.ds(pl.multiple_of(g * 512 + i * 64, 64), 64), :]
+    def fix_before_last(place, value):
+        at = block_at(8, *place)
+        r7[at, :] = r7[at, :] - value
+        d7[at, :] = d7[at, :] - (1.0 / THETA) * (inv7[at, :] * value)
+
+    apply(d7, o7, 8, lambda: blocks(8, before_last), fix_before_last)
+
+    def write(at, value):
+        i = lax.div(at.start, 64)
+        rows = pl.ds(pl.multiple_of(lax.rem(i, 8) * 64, 64), 64)
+        out[rows, pl.ds(pl.multiple_of(lax.div(i, 8) * LANES, LANES), LANES)] = value
+
+    smooth_second(inv7, r7, d7, x7, o7, 8, write)
 
 
 def per_device(rhs_local, stretch):
@@ -943,7 +967,7 @@
         compiler_params=pltpu.CompilerParams(
             collective_id=0, has_side_effects=True, vmem_limit_bytes=32 * 1024 * 1024
         ),
-    )(rhs_local.reshape(nodes, elems), stretch)
+    )(pltpu.with_memory_space_constraint(rhs_local.reshape(nodes, elems), pltpu.HBM), pltpu.with_memory_space_constraint(stretch, pltpu.HBM))
     return out.reshape(rhs_local.shape)
 
 

time: 80.6 us -> 76.3 us (0.947)
  Pallas kernels: 77.9 us -> 75.3 us
  local copies, waits for them, and re-layouts: 2.52 us -> 0.8 us
    pallas_call x1, Pallas kernels: 77.9 us -> 75.3 us  [per_device(): pl.pallas_call(functools.partial(kernel, nz, nr), out_shape=jax.ShapeDtyp...]
    unnamed x5 -> x1, local copies, waits for them, and re-layouts: 2.52 us -> 0.8 us
where the time goes in v5:
time: 76.3 us; the launch traced here: 76.1 us
  Pallas kernels  75.3 us (99%)
  local copies, waits for them, and re-layouts  0.8 us (1%)
    pallas_call x1, Pallas kernels, per_device(): pl.pallas_call(functools.partial(kernel, nz, nr), out_shape=jax.ShapeDtyp...  75.3 us

profile of v5, /device:TPU:1, one launch (start us, length us, event | category | flops | bytes accessed | tf_op | source)
XLA Modules:
  0.0 76.1 jit_solution(8419537980308163982)
XLA Ops:
  0.0 75.3 %shard_map.28 = f32[512,256]{1,0:T(8,128)S(1)} custom-call(f32[512,256]{1,0:T(8,128)} %bitcast.3, f32[3,256]{1,0:T(4,128)} %stretch_in.1), custom_call_target="tpu_custom_call" | custom-call | tf_op jit(solution)/shard_map/pallas_call | solution.py:929
  75.3 0.8 %copy.4 = f32[8,8,8,256]{3,2,1,0:T(8,128)} copy(f32[8,8,8,256]{3,2,1,0:T(8,128)S(1)} %bitcast.2) | data formatting | bytes 1048576

commit v6 on v5

--- a/solution.py
+++ b/solution.py
@@ -224,6 +224,14 @@
         tab[rows8(b * 8), :] = block
     loads[0].wait()
 
+    def row_targets():
+        if nr != 32:
+            return [(o, lax.rem(row + o, nr)) for o in range(1, nr)]
+        y, x, core = lax.div(row, 8), lax.rem(lax.div(row, 2), 4), lax.rem(row, 2)
+        ys, xs, cores = [lax.rem(y + k, 4) * 8 for k in range(4)], [lax.rem(x + k, 4) * 2 for k in range(4)], [core, 1 - core]
+        order = sorted(range(1, 32), key=lambda o: -(min(o // 8, 4 - o // 8) + min(o // 2 % 4, 4 - o // 2 % 4)))
+        return [(o, ys[o // 8] + xs[o // 2 % 4] + cores[o % 2]) for o in order]
+
     def const(name, j=0):
         return tab[rows8((WHERE[name] + j) * 8), :]
 
@@ -293,7 +301,7 @@
         for iz in range(n):
             image[rows8(base + iz * n * 8), :] = c0 * got[iz]
 
-    def rest_values(field, image, n, g, iz, pairs):
+    def rest_values(field, image, n, g, iz, pairs, along=None):
         w, k = WK[n]
         base = (g * n + iz) * (n * 8)
         got = line(k, [field[rows8(base + ia * 8), :] for ia in range(n)], pairs)
@@ -307,7 +315,8 @@
             for j in range(n):
                 term = const(("k", n), j) * field[pl.ds(at + j, 1), :]
                 part = term if part is None else part + term
-            values.append((ia, (float(w[ia]) * scale) * (image[rows8(at), :] + c1 * got[ia] + c2 * part)))
+            first = image[rows8(at), :] if along is None else along[ia]
+            values.append((ia, (float(w[ia]) * scale) * (first + c1 * got[ia] + c2 * part)))
         return values
 
     def element(field, image, n, sums, left=None):
@@ -480,23 +489,33 @@
         bottom = jnp.concatenate([left_part(1), block(1, 1)], axis=1)
         return jnp.concatenate([top, bottom], axis=0)
 
-    def exchange(*fields):
-        turn = Round(*fields)
-        turn.pack()
-        turn.start(LATE_FIRST)
+    def assemble(field, n):
+        turn = Round(field)
+        for d, place in enumerate(corners(n)):
+            send_diag[d, rows8(turn.at_diag), :] = with_r(field[block_at(n, *place), :], n)
+        turn.start((4, 5, 6, 7))
+        device_sum(field, n)
+        pack_a(field, n, turn.at)
+        turn.start((0, 1))
+        pack_z(field, n, turn.at)
+        turn.start((2, 3))
         turn.finish()
 
     def apply(field, image, n, during, fix):
         turn = Round(image)
         ends = (0, n - 1)
+        for d, (g, iz) in enumerate(((1, n - 1), (0, 0))):
+            along = {}
+            for ia in ends:
+                got = line(WK[n][1], [field[block_at(n, g, j, ia), :] for j in range(n)], (0,))
+                along[ia] = coef[rows8(g * 24), :] * got[iz]
+            (_, first), (_, last) = rest_values(field, image, n, g, iz, (0,), along)
+            send_diag[2 * d, rows8(turn.at_diag), :] = with_r(last, n)
+            send_diag[2 * d + 1, rows8(turn.at_diag), :] = with_r(first, n)
+        turn.start((4, 5, 6, 7))
         for g in range(2):
             for ia in ends:
                 along_z(field, image, n, g, ia)
-        for d, (g, iz) in enumerate(((1, n - 1), (0, 0))):
-            (_, first), (_, last) = rest_values(field, image, n, g, iz, (0,))
-            send_diag[2 * d, rows8(turn.at_diag), :] = with_r(last, n)
-            send_diag[2 * d + 1, rows8(turn.at_diag), :] = with_r(first, n)
-        turn.start((4, 5, 6, 7))
 
         def outer(i):
             g, iz = split(i, n)
@@ -666,8 +685,7 @@
     element(d7, o7, 8, False, left=r7)
 
     restrict(o7, 8, 4, r3, t1, t2)
-    device_sum(r3, 4)
-    exchange(r3)
+    assemble(r3, 4)
     smooth_first(inv3, r3, d3, 4)
     smooth_second(inv3, r3, d3, x3, o3, 4)
     element(d3, o3, 4, False, left=r3)
@@ -784,11 +802,10 @@
     for half in range(2):
         row_box[0, pl.ds(half, 1), :] = sent[half]
 
-    @pl.loop(1, nr)
-    def _(o):
+    for o, target in row_targets():
         pltpu.make_async_remote_copy(
             src_ref=row_box.at[0], dst_ref=row_box.at[o], send_sem=row_send, recv_sem=row_recv,
-            device_id=(gz, lax.rem(row + o, nr)), device_id_type=mesh_ids,
+            device_id=(gz, target), device_id_type=mesh_ids,
         ).start()
 
     def wait_for(box, count, sem):

time: 76.3 us -> 75.9 us (level)
  no operation moved by 1% of the time
where the time goes in v6:
time: 75.9 us; the launch traced here: 75.8 us
  Pallas kernels  75 us (99%)
  local copies, waits for them, and re-layouts  0.8 us (1%)
    pallas_call x1, Pallas kernels, per_device(): pl.pallas_call(functools.partial(kernel, nz, nr), out_shape=jax.ShapeDtyp...  75 us

profile of v6, /device:TPU:1, one launch (start us, length us, event | category | flops | bytes accessed | tf_op | source)
XLA Modules:
  0.0 75.8 jit_solution(16423553488255604520)
XLA Ops:
  0.0 75.0 %shard_map.28 = f32[512,256]{1,0:T(8,128)S(1)} custom-call(f32[512,256]{1,0:T(8,128)} %bitcast.3, f32[3,256]{1,0:T(4,128)} %stretch_in.1), custom_call_target="tpu_custom_call" | custom-call | tf_op jit(solution)/shard_map/pallas_call | solution.py:946
  75.0 0.8 %copy.4 = f32[8,8,8,256]{3,2,1,0:T(8,128)} copy(f32[8,8,8,256]{3,2,1,0:T(8,128)S(1)} %bitcast.2) | data formatting | bytes 1048576

commit v7 on v6

--- a/solution.py
+++ b/solution.py
@@ -177,7 +177,7 @@
     nz, nr, rhs, stretch_in, out, stretch, tab,
     x7, d7, r7, inv7, o7, t1, t2, x3, d3, r3, inv3, o3, t3, x1, r1, coef,
     vertex, lifted, images, send, recv, send_diag, recv_diag, send_block, recv_block, send_point, recv_point, row_box, gz_box,
-    load_sem, send_sem, recv_sem, block_send, block_recv, point_send, point_recv, row_send, row_recv, gz_send, gz_recv,
+    load_sem, send_sem, recv_sem, block_send, block_recv, point_send, point_recv, row_met, gz_met, row_send, row_recv, gz_send, gz_recv,
 ):
     gz = lax.axis_index("gz")
     row = lax.axis_index("row")
@@ -193,21 +193,15 @@
         return jnp.where(cond, 1.0, 0.0).astype(jnp.float32)
 
     def at_device(dz, da):
-        return (lax.rem(gz + (dz + nz), nz), lax.rem(row + (da + nr), nr))
+        return (lax.rem(gz + dz % nz, nz), lax.rem(row + da % nr, nr))
 
     barrier = pltpu.get_barrier_semaphore()
-
-    @pl.loop(1, nr)
-    def _(o):
-        pl.semaphore_signal(barrier, inc=1, device_id=(gz, lax.rem(row + o, nr)), device_id_type=mesh_ids)
-
-    @pl.loop(1, nz)
-    def _(o):
-        pl.semaphore_signal(barrier, inc=1, device_id=(lax.rem(gz + o, nz), row), device_id_type=mesh_ids)
-
-    askew = [d for d in FAR_DIRS if d[0] != 0 and d[1] != 0]
-    for dz, da in askew:
+    for dz, da in DIRS:
         pl.semaphore_signal(barrier, inc=1, device_id=at_device(dz, da), device_id_type=mesh_ids)
+
+    def greet(sem, dz, da):
+        for sign in (1, -1):
+            pl.semaphore_signal(sem, inc=1, device_id=at_device(sign * dz, sign * da), device_id_type=mesh_ids)
 
     loads = [pltpu.make_async_copy(stretch_in, stretch, load_sem.at[2])]
     for g in range(2):
@@ -581,10 +575,12 @@
         send_block[rows8(k * 8), :] = jnp.where(sub % 2 == 0, rows, roll(rows, 64))
     first_round = Round(r7, inv7, inv3)
     first_round.pack()
-    pl.semaphore_wait(barrier, (nr - 1) + (nz - 1) + len(askew))
+    pl.semaphore_wait(barrier, len(DIRS))
     first_round.start(LATE_FIRST)
     stretch_copies = send_all(DIRS, send_block, recv_block, block_send, block_recv)
     first_round.finish()
+    greet(row_met.at[0], 0, 2)
+    greet(gz_met.at[0], 2, 0)
 
     def invert(inv, n):
         keep = jnp.concatenate([live(n)] * 8, axis=0)
@@ -682,12 +678,20 @@
 
     smooth_first(inv7, r7, d7, 8)
     smooth_second(inv7, r7, d7, x7, o7, 8)
+    pl.semaphore_wait(row_met.at[0], 2)
+    pl.semaphore_wait(gz_met.at[0], 2)
+    greet(row_met.at[1], 0, 4)
+    greet(gz_met.at[1], 4, 0)
     element(d7, o7, 8, False, left=r7)
 
     restrict(o7, 8, 4, r3, t1, t2)
     assemble(r3, 4)
+    pl.semaphore_wait(row_met.at[1], 2)
+    pl.semaphore_wait(gz_met.at[1], 2)
+    greet(row_met.at[2], 0, 8)
     smooth_first(inv3, r3, d3, 4)
     smooth_second(inv3, r3, d3, x3, o3, 4)
+    pl.semaphore_wait(row_met.at[2], 2)
     element(d3, o3, 4, False, left=r3)
 
     restrict(o3, 4, 2, r1, t3, t2)
@@ -976,6 +980,8 @@
             pltpu.SemaphoreType.DMA((8,)),
             pltpu.SemaphoreType.DMA((len(FAR_DIRS),)),
             pltpu.SemaphoreType.DMA((len(FAR_DIRS),)),
+            pltpu.SemaphoreType.REGULAR((3,)),
+            pltpu.SemaphoreType.REGULAR((2,)),
             pltpu.SemaphoreType.DMA,
             pltpu.SemaphoreType.DMA,
             pltpu.SemaphoreType.DMA,

time: 75.9 us -> 74.6 us (0.983)
  Pallas kernels: 75 us -> 73.6 us
    pallas_call x1, Pallas kernels: 75 us -> 73.6 us  [per_device(): pl.pallas_call(functools.partial(kernel, nz, nr), out_shape=jax.ShapeDtyp...]
where the time goes in v7:
time: 74.6 us; the launch traced here: 74.4 us
  Pallas kernels  73.6 us (99%)
  local copies, waits for them, and re-layouts  0.8 us (1%)
    pallas_call x1, Pallas kernels, per_device(): pl.pallas_call(functools.partial(kernel, nz, nr), out_shape=jax.ShapeDtyp...  73.6 us

profile of v7, /device:TPU:1, one launch (start us, length us, event | category | flops | bytes accessed | tf_op | source)
XLA Modules:
  0.0 74.4 jit_solution(7827005248832499600)
XLA Ops:
  0.0 73.6 %shard_map.28 = f32[512,256]{1,0:T(8,128)S(1)} custom-call(f32[512,256]{1,0:T(8,128)} %bitcast.3, f32[3,256]{1,0:T(4,128)} %stretch_in.1), custom_call_target="tpu_custom_call" | custom-call | tf_op jit(solution)/shard_map/pallas_call | solution.py:950
  73.6 0.8 %copy.4 = f32[8,8,8,256]{3,2,1,0:T(8,128)} copy(f32[8,8,8,256]{3,2,1,0:T(8,128)S(1)} %bitcast.2) | data formatting | bytes 1048576

commit v8 on v7

--- a/solution.py
+++ b/solution.py
@@ -454,6 +454,14 @@
             for place in self.places():
                 unpack(*place, fix)
 
+        def finish_but_last(self):
+            for copy in self.copies:
+                copy.wait()
+            *most, last = self.places()
+            for place in most:
+                unpack(*place)
+            return lambda: unpack(*last)
+
     LATE_FIRST = (4, 5, 6, 7, 0, 1, 2, 3)
 
     def send_all(dirs, src, dst, sends, recvs):
@@ -578,7 +586,7 @@
     pl.semaphore_wait(barrier, len(DIRS))
     first_round.start(LATE_FIRST)
     stretch_copies = send_all(DIRS, send_block, recv_block, block_send, block_recv)
-    first_round.finish()
+    unpack_inv3 = first_round.finish_but_last()
     greet(row_met.at[0], 0, 2)
     greet(gz_met.at[0], 2, 0)
 
@@ -590,8 +598,9 @@
 
         blocks(n, body)
 
-    invert(inv7, 8)
-    invert(inv3, 4)
+    def level_3_diagonal():
+        unpack_inv3()
+        invert(inv3, 4)
 
     def smooth_first(inv, r, d, n):
         def body(at):
@@ -599,7 +608,7 @@
 
         blocks(n, body)
 
-    def smooth_second(inv, r, d, x, image, n, result=None):
+    def smooth_second(inv, r, d, x, image, n, result=None, beside=None):
         def body(at):
             step = d[at, :]
             left = r[at, :] - image[at, :]
@@ -625,7 +634,12 @@
             else:
                 x[at, :] = x[at, :] - change
 
-        apply(d, image, n, lambda: blocks(n, body), fix)
+        def during():
+            blocks(n, body)
+            if beside is not None:
+                beside()
+
+        apply(d, image, n, during, fix)
 
     def r_line(name, field, at, count):
         part = None
@@ -676,8 +690,15 @@
         loop(2 * nc, along_a, nf < 8)
         loop(2 * nf, along_z, nf < 8)
 
-    smooth_first(inv7, r7, d7, 8)
-    smooth_second(inv7, r7, d7, x7, o7, 8)
+    keep_7 = jnp.concatenate([live(8)] * 8, axis=0)
+
+    def invert_and_smooth(at):
+        inverse = jnp.where(keep_7, 1.0 / jnp.where(keep_7, inv7[at, :], 1.0), 0.0)
+        inv7[at, :] = inverse
+        d7[at, :] = (1.0 / THETA) * (inverse * r7[at, :])
+
+    blocks(8, invert_and_smooth)
+    smooth_second(inv7, r7, d7, x7, o7, 8, beside=level_3_diagonal)
     pl.semaphore_wait(row_met.at[0], 2)
     pl.semaphore_wait(gz_met.at[0], 2)
     greet(row_met.at[1], 0, 4)
@@ -860,8 +881,7 @@
     for half in range(2):
         gz_box[0, pl.ds(half, 1), :] = total[half]
 
-    @pl.loop(1, nz)
-    def _(o):
+    for o in sorted(range(1, nz), key=lambda o: -min(o, nz - o)):
         pltpu.make_async_remote_copy(
             src_ref=gz_box.at[0], dst_ref=gz_box.at[o], send_sem=gz_send, recv_sem=gz_recv,
             device_id=(lax.rem(gz + o, nz), row), device_id_type=mesh_ids,
@@ -870,8 +890,6 @@
     lifted_round.finish()
     wait_for(gz_box, nz, gz_recv)
     total = total_of(gz_box, nz)
-    wait_for(row_box, nr, row_send)
-    wait_for(gz_box, nz, gz_send)
 
     system = []
     for half in range(2):
@@ -934,6 +952,8 @@
         out[rows, pl.ds(pl.multiple_of(lax.div(i, 8) * LANES, LANES), LANES)] = value
 
     smooth_second(inv7, r7, d7, x7, o7, 8, write)
+    wait_for(row_box, nr, row_send)
+    wait_for(gz_box, nz, gz_send)
 
 
 def per_device(rhs_local, stretch):

time: 74.6 us -> 74.3 us (level)
  no operation moved by 1% of the time
where the time goes in v8:
time: 74.3 us; the launch traced here: 74.2 us
  Pallas kernels  73.4 us (99%)
  local copies, waits for them, and re-layouts  0.8 us (1%)
    pallas_call x1, Pallas kernels, per_device(): pl.pallas_call(functools.partial(kernel, nz, nr), out_shape=jax.ShapeDtyp...  73.4 us

profile of v8, /device:TPU:1, one launch (start us, length us, event | category | flops | bytes accessed | tf_op | source)
XLA Modules:
  0.0 74.2 jit_solution(3642203653329540926)
XLA Ops:
  0.0 73.4 %shard_map.28 = f32[512,256]{1,0:T(8,128)S(1)} custom-call(f32[512,256]{1,0:T(8,128)} %bitcast.3, f32[3,256]{1,0:T(4,128)} %stretch_in.1), custom_call_target="tpu_custom_call" | custom-call | tf_op jit(solution)/shard_map/pallas_call | solution.py:970
  73.4 0.8 %copy.4 = f32[8,8,8,256]{3,2,1,0:T(8,128)} copy(f32[8,8,8,256]{3,2,1,0:T(8,128)S(1)} %bitcast.2) | data formatting | bytes 1048576
